TPU v7x, 128 devices: a whole 4x4x4 slice. The times are simulated.
128 devices in a mesh: dp: 32 (over z, y, core), tp: 4 (over x).
Axes of the slice: x: 4, y: 4, z: 4, core: 2. Of those that a mesh axis runs over, the one named last changes fastest.
Arguments:
- hidden_in: bfloat16 [64, 512, 768], P('dp', 'tp'), may hold values from -6 to 6
- reset: int32 [64], P('dp'), may hold values from 0 to 1, as said below
- w_qkv: bfloat16 [768, 2304], P(('dp', 'tp')), may hold values from -0.21875 to 0.21875
- w_attn_out: bfloat16 [768, 768], P(('dp', 'tp')), may hold values from -0.3125 to 0.3125
- norm_gains: bfloat16 [2, 768], P(None, ('dp', 'tp')), may hold values from 0.5 to 1.5
- norm_biases: bfloat16 [2, 768], P(None, ('dp', 'tp')), may hold values from -2 to 2
- memory_tokens: bfloat16 [2, 10, 768], P(None, None, ('dp', 'tp')), may hold values from -6 to 6
- w_in: bfloat16 [768, 3072], P('dp', 'tp'), may hold values from -0.21875 to 0.21875
- w_out: bfloat16 [3072, 768], P('tp', 'dp'), may hold values from -0.109375 to 0.109375
- grad_hidden: bfloat16 [64, 512, 768], P('dp', 'tp'), may hold values from -6 to 6
- grad_memory: bfloat16 [64, 20, 768], P('dp', 'tp'), may hold values from -6 to 6
Outputs:
- hidden_out: bfloat16 [64, 512, 768], P('dp', 'tp')
- memory_out: bfloat16 [64, 20, 768], P('dp', 'tp')
- grad_in: float32 [64, 512, 768], P('dp', 'tp')
- grad_qkv: float32 [768, 2304], P(('dp', 'tp'))
- grad_attn_out: float32 [768, 768], P(('dp', 'tp'))
- grad_gains: float32 [2, 768], P(None, ('dp', 'tp'))
- grad_biases: float32 [2, 768], P(None, ('dp', 'tp'))
- grad_memory_tokens: float32 [2, 10, 768], P(None, None, ('dp', 'tp'))
- grad_w_in: float32 [768, 3072], P('dp', 'tp')
- grad_w_out: float32 [3072, 768], P('tp', 'dp')
Inputs may be any that keep to these rules, and one draw needn't show every extreme that they name: reset is 1 at the first segment of every index of dp; each index of dp holds one chain of exactly 2 segments: reset is 1 at its first segment and 0 at its second.
All inputs are finite; a program needn't handle non-finite values.
Results may differ from a plain program's by a relative error of at most 0.017.
Values may be sent and summed in bfloat16 or wider, within the bound.
A program may use at most 128 MiB of HBM per device.

v0:
```python
import jax
import jax.numpy as jnp
from jax import lax
from jax.sharding import PartitionSpec as P

D = 768
HEADS = 12
HEAD_DIM = 64
MEM = 10


EPSILON = 1e-05
INV_ROOT_TWO = 0.7071067811865476
INV_ROOT_TWOPI = 0.3989422804014327


def passed_along(value, axis, steps):
    count = lax.axis_size(axis)
    initial, last = (max(0, -steps), min(count, count - steps))
    return lax.ppermute(value, axis, [(source, source + steps) for source in range(initial, last)])


def norm_forward(inputs, gain, offset):
    centre = jnp.mean(inputs, -1, keepdims=True)
    centred = inputs - centre
    spread = jnp.mean(centred * centred, -1, keepdims=True)
    inverse = lax.rsqrt(spread + EPSILON)
    normed = centred * inverse
    return (normed * gain + offset, normed, inverse)


def norm_backward(upstream, normed, inverse, gain):
    scaled = upstream * gain
    first_mean = jnp.mean(scaled, -1, keepdims=True)
    second_mean = jnp.mean(scaled * normed, -1, keepdims=True)
    return inverse * (scaled - first_mean - normed * second_mean)


def gelu_value(inputs):
    return 0.5 * inputs * (1.0 + lax.erf(inputs * INV_ROOT_TWO))


def gelu_slope(inputs):
    return (
        0.5 * (1.0 + lax.erf(inputs * INV_ROOT_TWO))
        + inputs * jnp.exp(-0.5 * inputs * inputs) * INV_ROOT_TWOPI
    )


def body(
    hidden_in,
    reset,
    w_qkv,
    w_attn_out,
    norm_gains,
    norm_biases,
    memory_tokens,
    w_in,
    w_out,
    grad_hidden,
    grad_memory,
):
    groups = lax.axis_size("tp")
    place = lax.axis_index("tp")
    qkv_full, proj_full, gains_full, biases_full, tokens_full = (
        lax.all_gather(w_qkv, ("dp", "tp"), axis=0, tiled=True),
        lax.all_gather(w_attn_out, ("dp", "tp"), axis=0, tiled=True),
        lax.all_gather(norm_gains, ("dp", "tp"), axis=1, tiled=True),
        lax.all_gather(norm_biases, ("dp", "tp"), axis=1, tiled=True),
        lax.all_gather(memory_tokens, ("dp", "tp"), axis=2, tiled=True),
    )
    in_full, out_full = (
        lax.all_gather(w_in, "dp", axis=0, tiled=True),
        lax.all_gather(w_out, "dp", axis=1, tiled=True),
    )
    gains = gains_full.astype(jnp.float32)
    biases = biases_full.astype(jnp.float32)
    seg_count, own_rows, width = hidden_in.shape
    memory_rows = 2 * MEM // groups
    block_rows = own_rows + memory_rows
    key_rows = block_rows * groups
    flat_tokens = tokens_full.reshape(2 * MEM, width)
    own_initial = lax.dynamic_slice_in_dim(flat_tokens, place * memory_rows, memory_rows, 0)
    reading = place < groups // 2

    def forward_step(carry, inputs):
        segment, flag = inputs
        arrived = passed_along(carry, "tp", -(groups // 2))
        carried = jnp.logical_and(reading, flag == 0)
        memory_in = jnp.where(carried, arrived, own_initial)
        block = jnp.concatenate([segment, memory_in], 0)
        everyone = lax.all_gather(block, "tp", axis=0, tiled=True)
        queries = jnp.dot(block, qkv_full[:, :D], preferred_element_type=jnp.float32).astype(
            jnp.bfloat16
        )
        keyvals = jnp.dot(everyone, qkv_full[:, D:], preferred_element_type=jnp.float32).astype(
            jnp.bfloat16
        )
        query_heads = queries.reshape(block_rows, HEADS, HEAD_DIM)
        key_heads = keyvals[:, :D].reshape(key_rows, HEADS, HEAD_DIM)
        value_heads = keyvals[:, D:].reshape(key_rows, HEADS, HEAD_DIM)
        scores = (
            jnp.einsum("qhd,khd->hqk", query_heads, key_heads, preferred_element_type=jnp.float32)
            * 0.125
        )
        row_max = jnp.max(scores, -1, keepdims=True)
        raised = jnp.exp(scores - row_max)
        totals = jnp.sum(raised, -1, keepdims=True)
        probs_low = (raised / totals).astype(jnp.bfloat16)
        logsum = row_max + jnp.log(totals)
        mixed = jnp.einsum(
            "hqk,khd->qhd", probs_low, value_heads, preferred_element_type=jnp.float32
        )
        mixed = mixed.reshape(block_rows, D).astype(jnp.bfloat16)
        attended = jnp.dot(mixed, proj_full, preferred_element_type=jnp.float32)
        first, normed_one, inverse_one = norm_forward(
            block.astype(jnp.float32) + attended, gains[0], biases[0]
        )
        shared = lax.all_gather(first.astype(jnp.bfloat16), "tp", axis=0, tiled=True)
        hidden = jnp.dot(shared, in_full, preferred_element_type=jnp.float32)
        active = gelu_value(hidden).astype(jnp.bfloat16)
        branch = lax.psum_scatter(
            jnp.dot(active, out_full, preferred_element_type=jnp.float32).astype(jnp.bfloat16),
            "tp",
            scatter_dimension=0,
            tiled=True,
        ).astype(jnp.float32)
        final, normed_two, inverse_two = norm_forward(first + branch, gains[1], biases[1])
        final_low = final.astype(jnp.bfloat16)
        kept = (
            block,
            queries,
            keyvals,
            logsum,
            mixed,
            normed_one,
            inverse_one,
            shared,
            hidden,
            normed_two,
            inverse_two,
        )
        return (final_low[own_rows:], (final_low, kept))

    start_carry = jnp.zeros((memory_rows, width), jnp.bfloat16)
    _, (outputs, kept) = lax.scan(forward_step, start_carry, (hidden_in, reset))
    (
        block,
        queries,
        keyvals,
        logsum,
        mixed,
        normed_one,
        inverse_one,
        shared,
        hidden,
        normed_two,
        inverse_two,
    ) = kept
    upstream = jnp.concatenate([grad_hidden, grad_memory], 1).astype(jnp.float32)
    gain_two = jnp.sum(upstream * normed_two, (0, 1))
    bias_two = jnp.sum(upstream, (0, 1))
    into_final = norm_backward(upstream, normed_two, inverse_two, gains[1])
    branch_all = lax.all_gather(into_final.astype(jnp.bfloat16), "tp", axis=1, tiled=True)
    active = gelu_value(hidden).astype(jnp.bfloat16)
    grad_down = jnp.einsum("skf,skd->fd", active, branch_all, preferred_element_type=jnp.float32)
    grad_active = jnp.einsum(
        "skd,fd->skf", branch_all, out_full, preferred_element_type=jnp.float32
    )
    grad_units = (grad_active * gelu_slope(hidden)).astype(jnp.bfloat16)
    grad_up = jnp.einsum("skd,skf->df", shared, grad_units, preferred_element_type=jnp.float32)
    partial_first = jnp.einsum(
        "skf,df->skd", grad_units, in_full, preferred_element_type=jnp.float32
    )
    into_first = (
        lax.psum_scatter(
            partial_first.astype(jnp.bfloat16), "tp", scatter_dimension=1, tiled=True
        ).astype(jnp.float32)
        + into_final
    )
    gain_one = jnp.sum(into_first * normed_one, (0, 1))
    bias_one = jnp.sum(into_first, (0, 1))
    into_sum = norm_backward(into_first, normed_one, inverse_one, gains[0])
    sum_low = into_sum.astype(jnp.bfloat16)
    grad_proj = jnp.einsum("sqe,sqd->ed", mixed, sum_low, preferred_element_type=jnp.float32)
    grad_mixed = jnp.einsum(
        "sqd,ed->sqe", sum_low, proj_full, preferred_element_type=jnp.float32
    ).astype(jnp.bfloat16)

    def attend_back(inputs):
        query_seg, keyval_seg, logsum_seg, grad_seg = inputs
        query_heads = query_seg.reshape(block_rows, HEADS, HEAD_DIM)
        key_heads = keyval_seg[:, :D].reshape(key_rows, HEADS, HEAD_DIM)
        value_heads = keyval_seg[:, D:].reshape(key_rows, HEADS, HEAD_DIM)
        scores = (
            jnp.einsum("qhd,khd->hqk", query_heads, key_heads, preferred_element_type=jnp.float32)
            * 0.125
        )
        probs = jnp.exp(scores - logsum_seg)
        probs_low = probs.astype(jnp.bfloat16)
        grad_heads = grad_seg.reshape(block_rows, HEADS, HEAD_DIM)
        grad_values = jnp.einsum(
            "hqk,qhd->khd", probs_low, grad_heads, preferred_element_type=jnp.float32
        )
        grad_probs = jnp.einsum(
            "qhd,khd->hqk", grad_heads, value_heads, preferred_element_type=jnp.float32
        )
        row_term = jnp.sum(probs * grad_probs, -1, keepdims=True)
        grad_scores = (probs * (grad_probs - row_term)).astype(jnp.bfloat16)
        grad_query = (
            jnp.einsum("hqk,khd->qhd", grad_scores, key_heads, preferred_element_type=jnp.float32)
            * 0.125
        )
        grad_key = (
            jnp.einsum("hqk,qhd->khd", grad_scores, query_heads, preferred_element_type=jnp.float32)
            * 0.125
        )
        key_terms = jnp.concatenate(
            [grad_key.reshape(key_rows, D), grad_values.reshape(key_rows, D)], -1
        )
        return (grad_query.reshape(block_rows, D).astype(jnp.bfloat16), key_terms)

    grad_queries, key_terms = lax.map(attend_back, (queries, keyvals, logsum, grad_mixed))
    own_keyvals = lax.psum_scatter(
        key_terms.astype(jnp.bfloat16), "tp", scatter_dimension=1, tiled=True
    )
    grad_projected = jnp.concatenate([grad_queries, own_keyvals], -1)
    grad_weight_qkv = jnp.einsum(
        "sqd,sqe->de", block, grad_projected, preferred_element_type=jnp.float32
    )
    grad_rows = into_sum + jnp.einsum(
        "sqe,de->sqd", grad_projected, qkv_full, preferred_element_type=jnp.float32
    )
    grad_input = grad_rows[:, :own_rows]
    weighting = jnp.where(reading, reset.astype(jnp.float32), jnp.ones((seg_count,), jnp.float32))
    memory_grad = jnp.sum(weighting[:, None, None] * grad_rows[:, own_rows:], 0)
    token_grads = jnp.zeros((2 * MEM, width), jnp.float32)
    token_grads = lax.dynamic_update_slice_in_dim(token_grads, memory_grad, place * memory_rows, 0)
    token_grads = token_grads.reshape(2, MEM, width)
    gain_grads = jnp.stack([gain_one, gain_two])
    bias_grads = jnp.stack([bias_one, bias_two])
    qkv_share, proj_share, gain_share, bias_share, token_share = (
        lax.psum_scatter(grad_weight_qkv, ("dp", "tp"), scatter_dimension=0, tiled=True),
        lax.psum_scatter(grad_proj, ("dp", "tp"), scatter_dimension=0, tiled=True),
        lax.psum_scatter(gain_grads, ("dp", "tp"), scatter_dimension=1, tiled=True),
        lax.psum_scatter(bias_grads, ("dp", "tp"), scatter_dimension=1, tiled=True),
        lax.psum_scatter(token_grads, ("dp", "tp"), scatter_dimension=2, tiled=True),
    )
    up_share, down_share = (
        lax.psum_scatter(
            grad_up.astype(jnp.bfloat16), "dp", scatter_dimension=0, tiled=True
        ).astype(jnp.float32),
        lax.psum_scatter(
            grad_down.astype(jnp.bfloat16), "dp", scatter_dimension=1, tiled=True
        ).astype(jnp.float32),
    )
    return (
        outputs[:, :own_rows],
        outputs[:, own_rows:],
        grad_input,
        qkv_share,
        proj_share,
        gain_share,
        bias_share,
        token_share,
        up_share,
        down_share,
    )


def solution(mesh):
    return jax.shard_map(
        body,
        mesh=mesh,
        in_specs=(
            P("dp", "tp", None),
            P("dp"),
            P(("dp", "tp"), None),
            P(("dp", "tp"), None),
            P(None, ("dp", "tp")),
            P(None, ("dp", "tp")),
            P(None, None, ("dp", "tp")),
            P("dp", "tp"),
            P("tp", "dp"),
            P("dp", "tp", None),
            P("dp", "tp", None),
        ),
        out_specs=(
            P("dp", "tp", None),
            P("dp", "tp", None),
            P("dp", "tp", None),
            P(("dp", "tp"), None),
            P(("dp", "tp"), None),
            P(None, ("dp", "tp")),
            P(None, ("dp", "tp")),
            P(None, None, ("dp", "tp")),
            P("dp", "tp"),
            P("tp", "dp"),
        ),
        check_vma=False,
    )
```

profile of v0, /device:TPU:1, one launch (start us, length us, event | category | flops | bytes accessed | tf_op | source)
XLA Modules:
  0.0 1502.5 jit_solution(9450545921494650170)
XLA Ops:
  10.1 67.8 %all_gather.30 = bf16[2,10,768]{1,0,2:T(2,128)(2,1)S(1)} all-gather(bf16[2,10,6]{1,0,2:T(2,128)(2,1)} %param.21), channel_id=1, replica_groups=mesh['dp'=32,'tp'=4] {'dp','tp'}, dimensions={2}, use_global_device_ids=true | all-gather | bytes 30960 | tf_op jit(solution)/shard_map/all_gather | solution.py:70
  78.3 46.6 %all-gather.4 = bf16[128,6,2]{1,2,0:T(2,128)(2,1)S(1)} all-gather(bf16[1,6,2]{1,2,0:T(2,128)(2,1)} %bitcast.243), channel_id=1, replica_groups=mesh['dp'=32,'tp'=4] {'dp','tp'}, dimensions={0}, use_global_device_ids=true | all-gather | bytes 3096 | tf_op jit(solution)/shard_map/all_gather | solution.py:68
  125.3 46.4 %all-gather.5 = bf16[128,6,2]{1,2,0:T(2,128)(2,1)S(1)} all-gather(bf16[1,6,2]{1,2,0:T(2,128)(2,1)} %bitcast.244), channel_id=1, replica_groups=mesh['dp'=32,'tp'=4] {'dp','tp'}, dimensions={0}, use_global_device_ids=true | all-gather | bytes 3096 | tf_op jit(solution)/shard_map/all_gather | solution.py:69
  180.3 10.8 all-gather.22.cloned.1.call-done
  197.7 36.2 %all-gather.16.cloned.1.call-done = bf16[768,768]{1,0:T(8,128)(2,1)} async-done(((bf16[24,768]{1,0:T(8,128)(2,1)}), bf16[768,768]{1,0:T(8,128)(2,1)}) %all-gather.16.cloned.1.call-update) | async-done | bytes 1179664 | tf_op jit(solution)/shard_map/all_gather | solution.py:73
  236.2 192.4 %while.46 = (s32[]{:T(128)}, bf16[5,768]{1,0:T(8,128)(2,1)S(1)}, bf16[2,133,768]{2,1,0:T(8,128)(2,1)}, bf16[2,133,768]{2,1,0:T(8,128)(2,1)}, bf16[2,133,768]{2,1...) while((s32[]{:T(128)}, bf16[5,768]{1,0:T(8,128)(2,1)S(1)}, ...), condition=%wide.region_8.9_spmd, body=%wide.region_0.8_spmd.sunk | while | flops 3059613952 | bytes 82481760 | solution.py:146
  243.7 13.8 all-gather.8
  271.3 10.5 all-gather.9
  286.6 34.8 %fusion.127 = bf16[136,768]{1,0:T(8,128)(2,1)S(1)} fusion(bf16[532,768]{1,0:T(8,128)(2,1)S(1)} %convolution_convert_fusion.6), kind=kCustom, calls=%all-reduce-scatter.clone.1 | all-reduce-scatter fusion | flops 417793 | bytes 1026560 | tf_op jit(solution)/shard_map/while
  338.6 13.7 all-gather.8
  366.0 10.5 all-gather.9
  381.3 37.7 %fusion.127 = bf16[136,768]{1,0:T(8,128)(2,1)S(1)} fusion(bf16[532,768]{1,0:T(8,128)(2,1)S(1)} %convolution_convert_fusion.6), kind=kCustom, calls=%all-reduce-scatter.clone.1 | all-reduce-scatter fusion | flops 417793 | bytes 1026560 | tf_op jit(solution)/shard_map/while
  433.1 28.1 %all-gather.20.cloned.1.call-done = bf16[2,532,768]{2,0,1:T(2,128)(2,1)} async-done(((bf16[2,133,768]{2,0,1:T(2,128)(2,1)}), bf16[2,532,768]{2,0,1:T(2,128)(2,1)}) %all-gather.20.cloned.1.call-update) | async-done | bytes 1634320 | tf_op jit(solution)/shard_map/all_gather | solution.py:164
  474.9 47.9 %all-reduce.19.cloned.1.call-done = bf16[2,532,768]{2,0,1:T(2,128)(2,1)} async-done(((bf16[2,532,768]{2,0,1:T(2,128)(2,1)}), bf16[2,532,768]{2,0,1:T(2,128)(2,1)}) %all-reduce.19.cloned.1.call-update) | async-done | bytes 1634320
  529.3 157.4 %while.47 = (s32[]{:T(128)}, bf16[2,133,768]{2,1,0:T(8,128)(2,1)}, bf16[2,532,1536]{2,0,1:T(2,128)(2,1)}, bf16[2,532,1536]{2,1,0:T(8,128)(2,1)}, bf16[2,133,768]...) while((s32[]{:T(128)}, bf16[2,133,768]{2,1,0:T(8,128)(2,1)}, ...), condition=%wide.region_16.17_spmd, body=%wide.region_14.16_spmd.sunk | while | flops 557883392 | bytes 71997728 | solution.py:223
  549.4 8.8 copy.167
  558.2 48.0 %dynamic_update_slice.92 = bf16[2,532,1536]{2,0,1:T(2,128)(2,1)} dynamic-update-slice(bf16[2,532,1536]{2,0,1:T(2,128)(2,1)} %get-tuple-element.780, bf16[1,532,1536]{2,0,1:T(2,128)(2,1)} %copy.167, s32[]{:T(128)} %get-tuple-element.778, s32[]{:T(128)} %constant.65.clone.1..sunk.1, s32[]{:T(128)} %constant.65.clone.1..sunk.1) | dynamic-update-slice | bytes 3268612 | tf_op jit(solution)/shard_map/while/body/jit(dynamic_update_index_in_dim)/dynamic_update_slice | solution.py:223
  636.9 48.0 %dynamic_update_slice.92 = bf16[2,532,1536]{2,0,1:T(2,128)(2,1)} dynamic-update-slice(bf16[2,532,1536]{2,0,1:T(2,128)(2,1)} %get-tuple-element.780, bf16[1,532,1536]{2,0,1:T(2,128)(2,1)} %copy.167, s32[]{:T(128)} %get-tuple-element.778, s32[]{:T(128)} %constant.65.clone.1..sunk.1, s32[]{:T(128)} %constant.65.clone.1..sunk.1) | dynamic-update-slice | bytes 3268612 | tf_op jit(solution)/shard_map/while/body/jit(dynamic_update_index_in_dim)/dynamic_update_slice | solution.py:223
  700.6 63.9 %all-reduce.21.cloned.1.call-done = bf16[2,532,1536]{2,0,1:T(2,128)(2,1)} async-done(((bf16[2,532,1536]{2,0,1:T(2,128)(2,1)}), bf16[2,532,1536]{2,0,1:T(2,128)(2,1)}) %all-reduce.21.cloned.1.call-update) | async-done | bytes 3268624
  773.5 368.1 %fusion.49 = (f32[8,2304]{1,0:T(8,128)S(1)}, f32[8,768]{1,0:T(8,128)S(1)}) fusion(f32[768,2304]{1,0:T(8,128)} %convolution_bitcast_fusion, f32[768,768]{1,0:T(8,128)S(1)} %convolution_bitcast_fusion.1), kind=kCustom, calls=%all-reduce-scatter.3 | all-reduce-scatter fusion | flops 3145729 | bytes 9535488
  1158.4 17.0 %collective-permute-start.42 = (f32[8,768]{1,0:T(8,128)S(1)}, f32[8,768]{1,0:T(8,128)S(1)}, u32[]{:S(2)}, u32[]{:S(2)}) collective-permute-start(f32[8,768]{1,0:T(8,128)S(1)} %get-tuple-element.411), channel_id=1, source_target_pairs={{0,9},{1,10},{2,11},{3,12},{4,13},{5,14},{6,15},{7,16},{8,17},{9,1... | collective-permute-start | bytes 73736
  1181.8 13.5 collective-permute-start.46
  1310.2 122.3 %all-reduce.23.cloned.1.call-done = (f32[2,768]{1,0:T(2,128)}, f32[2,768]{1,0:T(2,128)}, f32[2,10,768]{1,0,2:T(2,128)}) async-done(((f32[2,768]{1,0:T(2,128)}, f32[2,768]{1,0:T(2,128)}, f32[2,10,768]{1,0,2:T(2,128)}), (f32[2,768]{1,0:T(2,128)}, f32[2,768]{1,0:T(2,128)}, f32[2,10,768]{1,0,2:T(2,128)})) %all-reduce.23.cloned.1.call-update) | async-done | bytes 73744
  1473.6 21.1 %concatenate.15 = f32[262,2304]{1,0:T(8,128)S(1)} concatenate(f32[6,2304]{1,0:T(8,128)S(1)} %collective-permute-done.33, f32[8,2304]{1,0:T(8,128)} %copy-done.46, f32[8,2304]{1,0:T(8,128)} %copy-done.45, f32[8,2304]{1,0:T(8,128)} %copy-done.44, f32[8,2304]{1,0:T(8,128)} %copy-done.42, f32[8,2304]{1,0:T(8,128)} %copy-done.41, f32[8,2304]{1,0:T(8,128)} %copy-done.40, ...), dimensions={0} | concatenate | bytes 4829184
  (528 shorter events, 367.0 us)
Async XLA Ops:
  7.2 167.4 %all-gather.18.cloned.1.call-start = ((), (), s32[]{:S(2)}) async-start(), calls=%async_computation.3 | async-start | bytes 1216512 | tf_op jit(solution)/shard_map/all_gather | solution.py:74
  7.9 169.1 %all-gather.24.cloned.1.call-start = ((), (), s32[]{:S(2)}) async-start(), calls=%async_computation.8 | async-start | bytes 1585152 | tf_op jit(solution)/shard_map/all_gather | solution.py:67
  8.7 182.4 %all-gather.22.cloned.1.call-start = ((), (), s32[]{:S(2)}) async-start(), calls=%async_computation.7 | async-start | bytes 4755456 | tf_op jit(solution)/shard_map/all_gather | solution.py:66
  9.4 224.4 %all-gather.16.cloned.1.call-start = ((), (), s32[]{:S(2)}) async-start(), calls=%async_computation.2 | async-start | bytes 1216512 | tf_op jit(solution)/shard_map/all_gather | solution.py:73
  10.0 451.3 %all-gather.20.cloned.1.call-start = ((), (), s32[]{:S(2)}) async-start(), calls=%async_computation.4 | async-start | bytes 2042880 | tf_op jit(solution)/shard_map/all_gather | solution.py:164
  433.1 89.7 %all-reduce.19.cloned.1.call-start = ((), (), s32[]{:S(2)}) async-start(), calls=%async_computation.9 | async-start | bytes 3268608
  471.6 292.9 %all-reduce.21.cloned.1.call-start = ((), (), s32[]{:S(2)}) async-start(), calls=%async_computation.10 | async-start | bytes 6537216
  686.7 564.3 %reduce-scatter.11.cloned.1.call-start = ((), (), s32[]{:S(2)}) async-start(), calls=%async_computation.5 | async-start | bytes 1216512 | tf_op jit(solution)/shard_map/reduce_scatter | solution.py:250
  692.5 559.9 %reduce-scatter.13.cloned.1.call-start = ((), (), s32[]{:S(2)}) async-start(), calls=%async_computation.6 | async-start | bytes 1216512 | tf_op jit(solution)/shard_map/reduce_scatter | solution.py:253
  697.5 735.0 %all-reduce.23.cloned.1.call-start = ((), (), s32[]{:S(2)}) async-start(), calls=%async_computation.11 | async-start | bytes 1597440
  1150.6 24.8 %collective-permute-start.38 = (f32[8,768]{1,0:T(8,128)S(1)}, f32[8,768]{1,0:T(8,128)S(1)}, u32[]{:S(2)}, u32[]{:S(2)}) collective-permute-start(f32[8,768]{1,0:T(8,128)S(1)} %get-tuple-element.411), channel_id=1, source_target_pairs={{0,5},{1,6},{2,7},{3,8},{4,9},{5,10},{6,11},{7,12},{8,13},{9,14},{... | collective-permute-start | bytes 73736
  1151.9 26.9 %collective-permute-start.39 = (f32[8,768]{1,0:T(8,128)S(1)}, f32[8,768]{1,0:T(8,128)S(1)}, u32[]{:S(2)}, u32[]{:S(2)}) collective-permute-start(f32[8,768]{1,0:T(8,128)S(1)} %get-tuple-element.411), channel_id=1, source_target_pairs={{0,6},{1,7},{2,8},{3,9},{4,10},{5,11},{6,12},{7,13},{8,14},{9,15},... | collective-permute-start | bytes 73736
  1153.6 26.5 %collective-permute-start.40 = (f32[8,768]{1,0:T(8,128)S(1)}, f32[8,768]{1,0:T(8,128)S(1)}, u32[]{:S(2)}, u32[]{:S(2)}) collective-permute-start(f32[8,768]{1,0:T(8,128)S(1)} %get-tuple-element.411), channel_id=1, source_target_pairs={{0,7},{1,8},{2,9},{3,10},{4,11},{5,12},{6,13},{7,14},{8,15},{9,16}... | collective-permute-start | bytes 73736
  1156.2 25.6 %collective-permute-start.41 = (f32[8,768]{1,0:T(8,128)S(1)}, f32[8,768]{1,0:T(8,128)S(1)}, u32[]{:S(2)}, u32[]{:S(2)}) collective-permute-start(f32[8,768]{1,0:T(8,128)S(1)} %get-tuple-element.411), channel_id=1, source_target_pairs={{0,8},{1,9},{2,10},{3,11},{4,12},{5,13},{6,14},{7,15},{8,16},{9,17... | collective-permute-start | bytes 73736
  1158.4 36.9 %collective-permute-start.42 = (f32[8,768]{1,0:T(8,128)S(1)}, f32[8,768]{1,0:T(8,128)S(1)}, u32[]{:S(2)}, u32[]{:S(2)}) collective-permute-start(f32[8,768]{1,0:T(8,128)S(1)} %get-tuple-element.411), channel_id=1, source_target_pairs={{0,9},{1,10},{2,11},{3,12},{4,13},{5,14},{6,15},{7,16},{8,17},{9,1... | collective-permute-start | bytes 73736
  1175.4 21.6 %collective-permute-start.43 = (f32[8,768]{1,0:T(8,128)S(1)}, f32[8,768]{1,0:T(8,128)S(1)}, u32[]{:S(2)}, u32[]{:S(2)}) collective-permute-start(f32[8,768]{1,0:T(8,128)S(1)} %get-tuple-element.411), channel_id=1, source_target_pairs={{0,10},{1,11},{2,12},{3,13},{4,14},{5,15},{6,16},{7,17},{8,18},{9,... | collective-permute-start | bytes 73736
  1178.8 21.9 %collective-permute-start.44 = (f32[8,768]{1,0:T(8,128)S(1)}, f32[8,768]{1,0:T(8,128)S(1)}, u32[]{:S(2)}, u32[]{:S(2)}) collective-permute-start(f32[8,768]{1,0:T(8,128)S(1)} %get-tuple-element.411), channel_id=1, source_target_pairs={{0,11},{1,12},{2,13},{3,14},{4,15},{5,16},{6,17},{7,18},{8,19},{9,... | collective-permute-start | bytes 73736
  1180.1 25.9 %collective-permute-start.45 = (f32[8,768]{1,0:T(8,128)S(1)}, f32[8,768]{1,0:T(8,128)S(1)}, u32[]{:S(2)}, u32[]{:S(2)}) collective-permute-start(f32[8,768]{1,0:T(8,128)S(1)} %get-tuple-element.411), channel_id=1, source_target_pairs={{0,12},{1,13},{2,14},{3,15},{4,16},{5,17},{6,18},{7,19},{8,20},{9,... | collective-permute-start | bytes 73736
  1181.8 26.2 %collective-permute-start.46 = (f32[8,768]{1,0:T(8,128)S(1)}, f32[8,768]{1,0:T(8,128)S(1)}, u32[]{:S(2)}, u32[]{:S(2)}) collective-permute-start(f32[8,768]{1,0:T(8,128)S(1)} %get-tuple-element.411), channel_id=1, source_target_pairs={{0,13},{1,14},{2,15},{3,16},{4,17},{5,18},{6,19},{7,20},{8,21},{9,... | collective-permute-start | bytes 73736
  1299.9 133.9 %collective-permute-start.25 = (f32[8,2304]{1,0:T(8,128)S(1)}, f32[8,2304]{1,0:T(8,128)S(1)}, u32[]{:S(2)}, u32[]{:S(2)}) collective-permute-start(f32[8,2304]{1,0:T(8,128)S(1)} %get-tuple-element.410), channel_id=1, source_target_pairs={{0,24},{1,25},{2,26},{3,27},{4,28},{5,29},{6,30},{7,31},{8,32},{9,... | collective-permute-start | bytes 221192
  1301.2 136.2 %collective-permute-start.26 = (f32[8,2304]{1,0:T(8,128)S(1)}, f32[8,2304]{1,0:T(8,128)S(1)}, u32[]{:S(2)}, u32[]{:S(2)}) collective-permute-start(f32[8,2304]{1,0:T(8,128)S(1)} %get-tuple-element.410), channel_id=1, source_target_pairs={{0,25},{1,26},{2,27},{3,28},{4,29},{5,30},{6,31},{7,32},{8,33},{9,... | collective-permute-start | bytes 221192
  1302.5 138.2 %collective-permute-start.27 = (f32[8,2304]{1,0:T(8,128)S(1)}, f32[8,2304]{1,0:T(8,128)S(1)}, u32[]{:S(2)}, u32[]{:S(2)}) collective-permute-start(f32[8,2304]{1,0:T(8,128)S(1)} %get-tuple-element.410), channel_id=1, source_target_pairs={{0,26},{1,27},{2,28},{3,29},{4,30},{5,31},{6,32},{7,33},{8,34},{9,... | collective-permute-start | bytes 221192
  1305.8 141.5 %collective-permute-start.28 = (f32[8,2304]{1,0:T(8,128)S(1)}, f32[8,2304]{1,0:T(8,128)S(1)}, u32[]{:S(2)}, u32[]{:S(2)}) collective-permute-start(f32[8,2304]{1,0:T(8,128)S(1)} %get-tuple-element.410), channel_id=1, source_target_pairs={{0,27},{1,28},{2,29},{3,30},{4,31},{5,32},{6,33},{7,34},{8,35},{9,... | collective-permute-start | bytes 221192
  1308.9 141.8 %collective-permute-start.29 = (f32[8,2304]{1,0:T(8,128)S(1)}, f32[8,2304]{1,0:T(8,128)S(1)}, u32[]{:S(2)}, u32[]{:S(2)}) collective-permute-start(f32[8,2304]{1,0:T(8,128)S(1)} %get-tuple-element.410), channel_id=1, source_target_pairs={{0,28},{1,29},{2,30},{3,31},{4,32},{5,33},{6,34},{7,35},{8,36},{9,... | collective-permute-start | bytes 221192
  (142 other events, 2571.3 us)
Sparse Core Ops, SparseCore 0:
  10.3 46.7 all-gather.17
  59.9 63.3 all-gather.23
  126.2 64.8 all-gather.21
  193.2 40.5 all-gather.15
  433.2 28.0 all-gather.19
  471.7 51.0 all-reduce.18
  686.9 77.5 all-reduce.20
  768.5 75.7 reduce-scatter.10
  848.2 76.8 reduce-scatter.12
  1286.4 146.1 all-reduce.22
where the time goes:
time: 1530 us; the launch traced here: 1500 us
  blocking collectives  650 us (42%)
  waiting for transfers between devices  315 us (21%)
  local copies, waits for them, and re-layouts  236 us (15%)
  starting transfers between devices  183 us (12%)
  matrix products  75.3 us (5%)
  other arithmetic  23.5 us (2%)
  between operations  16.7 us (1%)
    unnamed x1, blocking collectives  368 us
    unnamed x77, waiting for transfers between devices  240 us
    unnamed x67, starting transfers between devices  176 us
    dynamic_update_slice x4, local copies, waits for them, and re-layouts, body(): lax.map(attend_back, (queries, keyvals, logsum, grad_mixed))  114 us
    while x2, blocking collectives  72.5 us
    all_gather x1, blocking collectives, body(): lax.all_gather(memory_tokens, ('dp', 'tp'), axis=2, tiled=True)  67.8 us
    unnamed x94, local copies, waits for them, and re-layouts  58.7 us
    all_gather x1, blocking collectives, body(): lax.all_gather(norm_gains, ('dp', 'tp'), axis=1, tiled=True)  46.6 us
  transfers between devices with their start and end apart: 78, of which 9 were waited for; matrix products, arithmetic and copies ran while one was open for 30% of the time, Pallas kernels for 0%

commit v1 on v0

v1 whole, which is shorter than its diff:
```python
import functools

import jax
import jax.numpy as jnp
import numpy as np
from jax import lax
from jax.experimental import pallas as pl
from jax.experimental.pallas import tpu as pltpu
from jax.sharding import PartitionSpec as P

D = 768
HALF = 384
MEM = 10
TOKENS = 64
OWN = 272
ROWS = 2 * OWN
TP = 4
SMALL = 128
ACOLS = 4 * HALF + SMALL
CUT = 768
EPSILON = 1e-05
INV_ROOT_TWO = 0.7071067811865476
INV_ROOT_TWOPI = 0.3989422804014327
EXP_SCALE = 0.125 * 1.4426950408889634
MASKED = -1e30
F32 = jnp.float32
BF16 = jnp.bfloat16
MESH = pl.DeviceIdType.MESH
NN = (((1,), (0,)), ((), ()))
NT = (((1,), (1,)), ((), ()))
TN = (((0,), (0,)), ((), ()))


def dot(a, b, dims=NN):
    return lax.dot_general(a, b, dims, preferred_element_type=F32)


def up16(n):
    return -(-n // 16) * 16


class Shape:
    def __init__(self, dp):
        self.dp = dp
        planes = dp // 2
        self.ny = int(round(planes**0.5))
        self.nz = planes // self.ny
        self.wrows = D // dp
        self.arows = D // (dp * TP)
        self.brows = 2 * self.wrows
        self.pr = up16(self.arows)
        self.fr = up16(self.wrows)


def selections(sh):
    pack = np.zeros((sh.brows, TP * 2 * sh.pr), np.float32)
    for c in range(2):
        for x in range(TP):
            for i in range(sh.arows):
                pack[c * sh.wrows + x * sh.arows + i, (x * 2 + c) * sh.pr + i] = 1
    small = np.zeros((48, SMALL), np.float32)
    for i in range(4):
        small[i, i] = 1
    for kind in range(2):
        for i in range(MEM):
            small[16 + 16 * kind + (i // 5) * 8 + i % 5, 4 + MEM * kind + i] = 1
    return pack, small


def norm_forward(inputs, gain, offset):
    centred = inputs - jnp.mean(inputs, -1, keepdims=True)
    spread = jnp.mean(centred * centred, -1, keepdims=True)
    inverse = lax.rsqrt(spread + EPSILON)
    normed = centred * inverse
    return normed * gain + offset, normed, inverse


def norm_backward(upstream, normed, inverse, gain):
    scaled = upstream * gain
    first_mean = jnp.mean(scaled, -1, keepdims=True)
    second_mean = jnp.mean(scaled * normed, -1, keepdims=True)
    return inverse * (scaled - first_mean - normed * second_mean)


def column_sum(a):
    return jnp.sum(a, 0, keepdims=True)


SCRATCH = {}


def scratch_of(sh):
    nz, ny, br = sh.nz, sh.ny, sh.brows
    s = {
        "p1": ((TP, 2, sh.pr, ACOLS), BF16),
        "f1": ((2, sh.fr, D), BF16),
        "wa": ((nz, ny, br, ACOLS), BF16),
        "wi": ((TP, nz, ny, br, HALF), BF16),
        "wt": ((TP, nz, ny, br, HALF), BF16),
        "wo": ((2, nz, ny, br, HALF), BF16),
        "par": ((8, D), F32),
        "x": ((ROWS, D), BF16),
        "gyt": ((TP * TOKENS, D), BF16),
        "gm": ((2, 8, D), F32),
        "qkv": ((9, ROWS, 128), BF16),
        "pt": ((6, ROWS, ROWS), BF16),
        "ot": ((3, 128, ROWS), BF16),
        "oc": ((ROWS, HALF), BF16),
        "oown": ((2, OWN, HALF), BF16),
        "h1": ((OWN, D), F32),
        "n1": ((OWN, D), F32),
        "inv1": ((OWN, 1), F32),
        "h1b": ((ROWS, D), BF16),
        "gl": ((TP, ROWS, HALF), BF16),
        "sl": ((TP, ROWS, HALF), BF16),
        "fs": ((OWN, D), F32),
        "fr": ((OWN, D), F32),
        "n2": ((OWN, D), F32),
        "yb": ((OWN, D), BF16),
        "mo": ((2, 8, D), F32),
        "hop": ((16, D), BF16),
        "dz": ((OWN, D), F32),
        "dfb": ((ROWS, D), BF16),
        "du": ((TP, ROWS, HALF), BF16),
        "dhs": ((OWN, D), F32),
        "dhr": ((OWN, D), F32),
        "dr": ((OWN, D), F32),
        "dab": ((ROWS, D), BF16),
        "doc": ((3, ROWS, 128), BF16),
        "dqkv": ((9, ROWS, 128), BF16),
        "ga": ((nz, ny, br, ACOLS), BF16),
        "gi": ((TP, nz, ny, br, HALF), BF16),
        "gt": ((TP, nz, ny, br, HALF), BF16),
        "gos": ((D // 2 // br if nz > 1 else 1, br if nz > 1 else HALF, HALF), BF16),
        "dxs": ((OWN, D), F32),
        "dxr": ((OWN, D), F32),
        "dxb": ((TP * TOKENS, D), BF16),
        "sg": ((48, D), F32),
        "e3": ((TP, 2, sh.pr, ACOLS), BF16),
        "r3": ((TP - 1, 2, sh.pr, ACOLS), BF16),
        "s4": ((2, sh.pr, ACOLS), F32),
        "sf": ((2, sh.wrows, D), F32),
    }
    if nz > 1:
        s["gos"] = ((nz // 2, ny, br, HALF), BF16)
    else:
        s["gos"] = ((1, 1, HALF, HALF), BF16)
    sizes = {"x": TP, "z": nz, "y": ny}
    for name, order, cols, axes in jobs_of():
        left = [a for a in axes]
        for step, axis in enumerate(order):
            left = [a for a in left if a != axis]
            dims = tuple(sizes[a] for a in left)
            s[f"r{step}_{name}"] = ((max(1, sizes[axis] - 1),) + dims + (br, cols.stop - cols.start), BF16)
            if step < len(order) - 1:
                s[f"s{step}_{name}"] = (dims + (br, cols.stop - cols.start), BF16)
    return s


def jobs_of():
    orders = [("z", "y", "x"), ("x", "z", "y"), ("y", "x", "z")]
    jobs = []
    for kind in ("t", "i"):
        for j in range(3):
            jobs.append((f"{kind}{j}", orders[j], slice(128 * j, 128 * j + 128), ("x", "z", "y")))
    jobs.append(("a0", ("z", "y"), slice(0, CUT), ("z", "y")))
    jobs.append(("a1", ("y", "z"), slice(CUT, ACOLS), ("z", "y")))
    return jobs


ARRAY = {"t": ("wt", "gt"), "i": ("wi", "gi"), "a": ("wa", "ga")}


def kernel(sh, names, *refs):
    xin, gin, gmem, pk, ff, packsel, smallsel = refs[:7]
    hout, mout, dxo, gao, gfo = refs[7:12]
    b = dict(zip(names, refs[12 : 12 + len(names)]))
    ssem, rsem, xsem, lsem = refs[12 + len(names) :]
    nz, ny, br, wr, pr = sh.nz, sh.ny, sh.brows, sh.wrows, sh.pr

    dp = lax.axis_index("dp")
    x = lax.axis_index("tp")
    core = dp % 2
    y = (dp // 2) % ny
    z = dp // (2 * ny)
    other = 1 - core
    chain = x // 2
    seg = jnp.where((x == 1) | (x == 2), 1, 0)
    at = {"x": x, "y": y, "z": z}
    size = {"x": TP, "y": ny, "z": nz}

    def device(x_=x, y_=y, z_=z, c_=core):
        return ((z_ * ny + y_) * 2 + c_, x_)

    def moved(axis, offset, core_=core):
        there = dict(at)
        there[axis] = (at[axis] + offset) % size[axis]
        return device(there["x"], there["y"], there["z"], core_)

    sibling = device(c_=other)
    counts = {"s": 0, "r": 0}
    sent = []

    def remote(src, dst, to):
        copy = pltpu.make_async_remote_copy(
            src_ref=src,
            dst_ref=dst,
            send_sem=ssem.at[counts["s"]],
            recv_sem=rsem.at[counts["r"]],
            device_id=to,
            device_id_type=MESH,
        )
        counts["s"] += 1
        counts["r"] += 1
        copy.start()
        sent.append(copy)
        return copy

    def arrived(copies):
        for copy in copies:
            copy.wait_recv()

    locals_ = [0]

    def local(src, dst):
        copy = pltpu.make_async_copy(src, dst, lsem.at[locals_[0]])
        locals_[0] += 1
        copy.start()
        return copy

    barrier = pltpu.get_barrier_semaphore()
    peers = [sibling]
    for o in range(1, TP):
        peers += [moved("x", o), moved("x", o, other)]
    for axis in ("y", "z"):
        for o in range(1, size[axis]):
            peers.append(moved(axis, o))
    for peer in peers:
        pl.semaphore_signal(barrier, inc=1, device_id=peer, device_id_type=MESH)
    pl.semaphore_wait(barrier, len(peers))

    pk_local = local(pk.at[core], b["p1"].at[x, core])
    ff_local = local(ff.at[core], b["f1"].at[core])
    pk_swap = remote(pk.at[other], b["p1"].at[x, core], sibling)
    ff_swap = remote(ff.at[other], b["f1"].at[core], sibling)

    conditional = []

    def to_device(src, dst, place, here, kind, send_slot):
        copy = pltpu.make_async_remote_copy(
            src_ref=src,
            dst_ref=dst,
            send_sem=xsem.at[kind, 8 + send_slot],
            recv_sem=here,
            device_id=device(x_=place[0], c_=place[1]),
            device_id_type=MESH,
        )
        same = (place[0] == x) & (place[1] == core)

        @pl.when(same)
        def _():
            pltpu.make_async_copy(src, dst, here).start()

        @pl.when(jnp.logical_not(same))
        def _():
            copy.start()

        conditional.append((same, copy))

    def from_device(dst, here):
        pltpu.make_async_copy(dst, dst, here).wait()

    def chip_of(k, s):
        return s + k * (3 - 2 * s)

    for s in range(2):
        for j in range(2):
            rows = pl.ds(TOKENS * j, TOKENS)
            to_device(
                xin.at[s, rows],
                b["x"].at[pl.ds(pl.multiple_of(OWN * j + TOKENS * x, 16), TOKENS)],
                (chip_of(core, s), j),
                xsem.at[0, x],
                0,
                2 * s + j,
            )
    for s in range(2):
        for j in range(2):
            rows = pl.ds(TOKENS * j, TOKENS)
            to_device(
                gin.at[s, rows],
                b["gyt"].at[pl.ds(pl.multiple_of(TOKENS * x, 16), TOKENS)],
                (chip_of(core, s), j),
                xsem.at[1, x],
                1,
                2 * s + j,
            )
        to_device(
            gmem.at[s],
            b["gm"].at[x % 2],
            (chip_of(core, s), x // 2),
            xsem.at[2, x % 2],
            2,
            s,
        )

    def index(axes, fixed):
        return tuple(fixed.get(a, slice(None)) for a in axes)

    def gather_step(job, step):
        name, order, cols, axes = job
        order = order[::-1]
        array = b[ARRAY[name[0]][0]]
        axis = order[step]
        fixed = {a: at[a] for a in order[step:]}
        part = array.at[index(axes, fixed) + (slice(None), cols)]
        return [remote(part, part, moved(axis, o)) for o in range(1, size[axis])]

    jobs = {j[0]: j for j in jobs_of()}
    ff_names = ["i0", "i1", "i2", "t0", "t1", "t2"]

    ff_local.wait()
    arrived([ff_swap])
    two = [b["f1"][c].astype(F32)[:wr] for c in range(2)]
    block = jnp.concatenate(two, 0).astype(BF16)
    b["wi"][x, z, y] = block[:, :HALF]
    b["wt"][x, z, y] = block[:, HALF:]

    pk_local.wait()
    arrived([pk_swap])
    mine = b["p1"].at[x]
    steps = [remote(mine, mine, moved("x", o)) for o in range(1, TP)]
    arrived(steps)
    b["wa"][z, y] = dot(packsel[...], b["p1"][...].reshape(TP * 2 * pr, ACOLS)).astype(BF16)
    first = {n: gather_step(jobs[n], 0) for n in ("a0", "a1")}
    ff_steps = {n: gather_step(jobs[n], 0) for n in ff_names}
    second = {}
    for n in ("a0", "a1"):
        arrived(first[n])
        second[n] = gather_step(jobs[n], 1)

    for i in range(TP):
        from_device(b["x"].at[pl.ds(pl.multiple_of(OWN * core + TOKENS * i, 16), TOKENS)], xsem.at[0, i])
    half = b["x"].at[pl.ds(pl.multiple_of(OWN * core, 16), TP * TOKENS)]
    x_swap = remote(half, half, sibling)

    for n in ff_names:
        arrived(ff_steps[n])
        ff_steps[n] = gather_step(jobs[n], 1)
    for n in ("a0", "a1"):
        arrived(second[n])
    wo_cols = slice(3 * HALF, 4 * HALF)
    wo_local = local(b["wa"].at[:, :, :, wo_cols], b["wo"].at[core])
    wo_swap = remote(b["wa"].at[:, :, :, wo_cols], b["wo"].at[core], sibling)
    for n in ff_names:
        arrived(ff_steps[n])
        ff_steps[n] = gather_step(jobs[n], 2)

    def attention_weight(n):
        return b["wa"][:, :, :, HALF * n : HALF * (n + 1)].reshape(D, HALF)

    small = b["wa"][:, :, :, 4 * HALF :].reshape(D, SMALL)
    chosen = dot(smallsel[...], small, NT)
    b["par"][...] = chosen[0:8]
    b["x"][OWN + 256 : OWN + 272] = chosen[32:48].astype(BF16)

    @pl.when(seg == 0)
    def _():
        b["x"][256:272] = chosen[16:32].astype(BF16)

    gains = [b["par"][i : i + 1] for i in range(2)]
    biases = [b["par"][2 + i : 3 + i] for i in range(2)]
    arrived([x_swap])

    hop_to = jnp.where(x == 0, 1, 2)
    hops = []
    for j in range(2):
        hops.append(
            pltpu.make_async_remote_copy(
                src_ref=b["hop"],
                dst_ref=b["x"].at[256:272],
                send_sem=xsem.at[6, j],
                recv_sem=xsem.at[6, 2],
                device_id=device(x_=hop_to, c_=j),
                device_id_type=MESH,
            )
        )

    @pl.when(seg == 1)
    def _():
        hops[0].wait_recv()

    own_rows = pl.ds(pl.multiple_of(OWN * core, 16), OWN)
    other_rows = pl.ds(pl.multiple_of(OWN * other, 16), OWN)

    for n in range(3):
        out = dot(b["x"][...], attention_weight(n)).astype(BF16)
        for p in range(3):
            b["qkv"][3 * n + p] = out[:, 128 * p : 128 * p + 128]

    def head_masks(hh):
        lane = lax.broadcasted_iota(jnp.int32, (ROWS, 128), 1)
        row = lax.broadcasted_iota(jnp.int32, (ROWS, 128), 0)
        inside = (lane // 64) == hh
        spare = lane == 64 * (1 - hh)
        memory = ((row >= 256) & (row < 272)) | (row >= OWN + 256)
        invalid = memory & (row % 8 >= 5)
        return inside, spare, invalid

    def forward_pair(p):
        qp, kp, vp = b["qkv"][p], b["qkv"][3 + p], b["qkv"][6 + p]
        vt = vp.T
        for hh in range(2):
            inside, spare, invalid = head_masks(hh)
            zero = jnp.zeros_like(kp)
            kmask = jnp.where(spare & invalid, jnp.full_like(kp, MASKED), zero)
            km = jnp.where(inside, kp, kmask)
            qm = jnp.where(inside, qp, jnp.where(spare, jnp.ones_like(qp), zero))
            scores = dot(km, qm, NT)
            peak = jnp.max(scores, 0, keepdims=True)
            raised = jnp.exp2((scores - peak) * EXP_SCALE)
            total = jnp.sum(raised, 0, keepdims=True)
            probs = (raised * (1.0 / total)).astype(BF16)
            b["pt"][2 * p + hh] = probs
            b["ot"][p, 64 * hh : 64 * hh + 64] = dot(vt[64 * hh : 64 * hh + 64], probs).astype(BF16)

    for p in range(3):
        forward_pair(p)
        b["oc"][:, 128 * p : 128 * p + 128] = b["ot"][p].T

    o_local = local(b["oc"].at[own_rows], b["oown"].at[core])
    o_swap = remote(b["oc"].at[other_rows], b["oown"].at[core], sibling)
    wo_local.wait()
    arrived([wo_swap])
    o_local.wait()
    arrived([o_swap])
    halves = []
    for h in range(2):
        w = b["wo"][h].reshape(D, HALF)
        halves.append(dot(b["oown"][0], w[:HALF]) + dot(b["oown"][1], w[HALF:]))
    attended = jnp.concatenate(halves, 1)
    h1, n1, inv1 = norm_forward(b["x"][own_rows].astype(F32) + attended, gains[0], biases[0])
    b["h1"][...] = h1
    b["n1"][...] = n1
    b["inv1"][...] = inv1
    b["h1b"][own_rows] = h1.astype(BF16)
    h_swap = remote(b["h1b"].at[own_rows], b["h1b"].at[own_rows], sibling)
    for n in ff_names[:3]:
        arrived(ff_steps[n])
    arrived([h_swap])

    def up_weight(t):
        return b["wi"][t].reshape(D, HALF)

    def down_weight(t):
        return b["wt"][t].reshape(D, HALF)

    @pl.loop(0, TP)
    def _(t):
        units = dot(b["h1b"][...], up_weight(t))
        erf = 0.5 * (1.0 + lax.erf(units * INV_ROOT_TWO))
        b["gl"][t] = (units * erf).astype(BF16)
        b["sl"][t] = (erf + units * jnp.exp(-0.5 * units * units) * INV_ROOT_TWOPI).astype(BF16)

    for n in ff_names[3:]:
        arrived(ff_steps[n])

    def partial_down(rows):
        return sum(dot(b["gl"][t, rows], down_weight(t), NT) for t in range(TP))

    b["fs"][...] = partial_down(other_rows)
    f_swap = remote(b["fs"], b["fr"], sibling)
    branch = partial_down(own_rows)
    arrived([f_swap])
    out, n2, inv2 = norm_forward(b["h1"][...] + branch + b["fr"][...], gains[1], biases[1])
    low = out.astype(BF16)
    b["yb"][...] = low
    row16 = lax.broadcasted_iota(jnp.int32, (16, D), 0)
    memory_out = jnp.where(row16 % 8 < 5, out[256:272], 0.0).astype(BF16)
    b["hop"][...] = memory_out
    b["mo"][...] = memory_out.astype(F32).reshape(2, 8, D)

    @pl.when((seg == 0) & (core == 1))
    def _():
        hops[0].start()
        hops[1].start()

    for i in range(TP):
        to_device(
            b["yb"].at[pl.ds(TOKENS * i, TOKENS)],
            hout.at[seg, pl.ds(pl.multiple_of(TOKENS * core, 16), TOKENS)],
            (i, chain),
            xsem.at[3, 2 * seg + core],
            3,
            i,
        )
    for i in range(2):
        to_device(b["mo"].at[i], mout.at[seg], (2 * core + i, chain), xsem.at[4, seg], 4, i)

    for i in range(TP):
        from_device(b["gyt"].at[pl.ds(TOKENS * i, TOKENS)], xsem.at[1, i])
    for i in range(2):
        from_device(b["gm"].at[i], xsem.at[2, i])
    upstream = jnp.concatenate([b["gyt"][...].astype(F32), b["gm"][...].reshape(16, D)], 0)
    b["sg"][...] = jnp.zeros((48, D), F32)
    b["sg"][1:2] = column_sum(upstream * n2)
    b["sg"][3:4] = column_sum(upstream)
    dz = norm_backward(upstream, n2, inv2, gains[1])
    b["dz"][...] = dz
    b["dfb"][own_rows] = dz.astype(BF16)
    df_swap = remote(b["dfb"].at[own_rows], b["dfb"].at[own_rows], sibling)
    arrived([df_swap])

    @pl.loop(0, TP)
    def _(t):
        b["du"][t] = (dot(b["dfb"][...], down_weight(t)) * b["sl"][t].astype(F32)).astype(BF16)

    def partial_up(rows):
        return sum(dot(b["du"][t, rows], up_weight(t), NT) for t in range(TP))

    b["dhs"][...] = partial_up(other_rows)
    dh_swap = remote(b["dhs"], b["dhr"], sibling)
    dh_own = partial_up(own_rows)
    b["dz"][...] = b["dz"][...] + dh_own

    @pl.loop(0, TP)
    def _(t):
        b["gt"][t] = dot(b["dfb"][...], b["gl"][t], TN).astype(BF16).reshape(nz, ny, br, HALF)

    def pick(axes, axis, place):
        return tuple(place if a == axis else slice(None) for a in axes)

    def scatter_send(job, step):
        name, order, cols, axes = job
        axis = order[step]
        left = [a for a in axes if a not in order[:step]]
        if step == 0:
            source = b[ARRAY[name[0]][1]]
            tail = (slice(None), cols)
        else:
            source = b[f"s{step - 1}_{name}"]
            tail = ()
        copies = []
        for o in range(1, size[axis]):
            there = (at[axis] + o) % size[axis]
            copies.append(
                remote(source.at[pick(left, axis, there) + tail], b[f"r{step}_{name}"].at[o - 1], moved(axis, o))
            )
        return copies

    def scatter_sum(job, step, copies):
        name, order, cols, axes = job
        axis = order[step]
        left = [a for a in axes if a not in order[:step]]
        arrived(copies)
        if step == 0:
            mine = b[ARRAY[name[0]][1]][pick(left, axis, at[axis]) + (slice(None), cols)]
        else:
            mine = b[f"s{step - 1}_{name}"][pick(left, axis, at[axis])]
        total = mine.astype(F32)
        for o in range(1, size[axis]):
            total = total + b[f"r{step}_{name}"][o - 1].astype(F32)
        if step < len(order) - 1:
            b[f"s{step}_{name}"][...] = total.astype(BF16)
        return total

    rs = {n: scatter_send(jobs[n], 0) for n in ("t0", "t1", "t2")}

    @pl.loop(0, TP)
    def _(t):
        b["gi"][t] = dot(b["h1b"][...], b["du"][t], TN).astype(BF16).reshape(nz, ny, br, HALF)

    rs.update({n: scatter_send(jobs[n], 0) for n in ("i0", "i1", "i2")})

    arrived([dh_swap])
    into_first = b["dz"][...] + b["dhr"][...]
    b["sg"][0:1] = column_sum(into_first * b["n1"][...])
    b["sg"][2:3] = column_sum(into_first)
    dr = norm_backward(into_first, b["n1"][...], b["inv1"][...], gains[0])
    b["dr"][...] = dr
    b["dab"][own_rows] = dr.astype(BF16)
    da_swap = remote(b["dab"].at[own_rows], b["dab"].at[own_rows], sibling)
    arrived([da_swap])

    def head_rows(ref, c):
        if nz > 1:
            return ref.at[pl.ds(c * (nz // 2), nz // 2)]
        return ref.at[:, :, pl.ds(pl.multiple_of(c * HALF, 16), HALF)]

    grad_mixed = 0.0
    for h in range(2):
        w = head_rows(b["wo"].at[h], core)[...].reshape(HALF, HALF)
        grad_mixed = grad_mixed + dot(b["dab"][:, HALF * h : HALF * (h + 1)], w, NT)
    for p in range(3):
        b["doc"][p] = grad_mixed[:, 128 * p : 128 * p + 128].astype(BF16)

    mixed_t = b["ot"][...].reshape(HALF, ROWS)

    def proj_grad(h):
        cols = pl.ds(pl.multiple_of(HALF * h, 128), HALF)
        return dot(mixed_t, b["dab"][:, cols]).astype(BF16).reshape(b["gos"].shape)

    def wo_part(c):
        return head_rows(b["ga"].at[:, :, :, wo_cols], c)

    b["gos"][...] = proj_grad(other)
    go_swap = remote(b["gos"], wo_part(core), sibling)
    wo_part(core)[...] = proj_grad(core)

    def backward_pair(p):
        qp, kp, vp, dop = b["qkv"][p], b["qkv"][3 + p], b["qkv"][6 + p], b["doc"][p]
        kt = kp.T
        dv = dk = 0.0
        dq = []
        for hh in range(2):
            inside, _, _ = head_masks(hh)
            zero = jnp.zeros_like(kp)
            grad_probs = dot(jnp.where(inside, vp, zero), dop, NT)
            low_probs = b["pt"][2 * p + hh]
            probs = low_probs.astype(F32)
            row_term = jnp.sum(probs * grad_probs, 0, keepdims=True)
            ds = (probs * (grad_probs - row_term)).astype(BF16)
            dv = dv + dot(low_probs, jnp.where(inside, dop, zero))
            dk = dk + dot(ds, jnp.where(inside, qp, zero))
            dq.append(dot(kt[64 * hh : 64 * hh + 64], ds))
        b["dqkv"][p] = (jnp.concatenate(dq, 0) * 0.125).T.astype(BF16)
        b["dqkv"][3 + p] = (dk * 0.125).astype(BF16)
        b["dqkv"][6 + p] = dv.astype(BF16)

    for p in range(3):
        backward_pair(p)
        for n in (("t0", "t1", "t2"), ("i0", "i1", "i2"), ())[p]:
            scatter_sum(jobs[n], 0, rs[n])
            rs[n] = scatter_send(jobs[n], 1)

    def joined(n, rows):
        return jnp.concatenate([b["dqkv"][3 * n + p, rows] for p in range(3)], 1)

    everyone = slice(None)
    for n in range(3):
        part = dot(b["x"][...], joined(n, everyone), TN).astype(BF16)
        b["ga"][:, :, :, HALF * n : HALF * (n + 1)] = part.reshape(nz, ny, br, HALF)
    rs["a0"] = scatter_send(jobs["a0"], 0)

    def partial_input(rows):
        return sum(dot(joined(n, rows), attention_weight(n), NT) for n in range(3))

    b["dxs"][...] = partial_input(other_rows)
    dx_swap = remote(b["dxs"], b["dxr"], sibling)
    dx = partial_input(own_rows) + b["dr"][...]
    arrived([dx_swap])
    dx = dx + b["dxr"][...]
    b["dxb"][...] = dx[:256].astype(BF16)
    for i in range(TP):
        to_device(
            b["dxb"].at[pl.ds(TOKENS * i, TOKENS)],
            dxo.at[seg, pl.ds(pl.multiple_of(TOKENS * core, 16), TOKENS)],
            (i, chain),
            xsem.at[5, 2 * seg + core],
            5,
            i,
        )

    @pl.when((core == 0) & (seg == 0))
    def _():
        b["sg"][16:32] = dx[256:272]

    @pl.when(core == 1)
    def _():
        b["sg"][32:48] = dx[256:272]

    small_grads = dot(b["sg"][...].astype(BF16), smallsel[...], TN).astype(BF16)
    b["ga"][:, :, :, 4 * HALF :] = small_grads.reshape(nz, ny, br, SMALL)
    arrived([go_swap])
    rs["a1"] = scatter_send(jobs["a1"], 0)

    for n in ("t0", "t1", "t2"):
        scatter_sum(jobs[n], 1, rs[n])
        rs[n] = scatter_send(jobs[n], 2)
    for n in ("a0", "a1"):
        scatter_sum(jobs[n], 0, rs[n])
        rs[n] = scatter_send(jobs[n], 1)
    for n in ("i0", "i1", "i2"):
        scatter_sum(jobs[n], 1, rs[n])
        rs[n] = scatter_send(jobs[n], 2)
    last = [scatter_sum(jobs[n], 1, rs[n]).astype(BF16) for n in ("a0", "a1")]
    for n, cols in zip(range(2), (slice(0, CUT), slice(CUT, ACOLS))):
        spread = dot(packsel[...], last[n], TN).astype(BF16)
        b["e3"][:, :, :, cols] = spread.reshape(TP, 2, pr, cols.stop - cols.start)
    steps = [remote(b["e3"].at[(x + o) % TP], b["r3"].at[o - 1], moved("x", o)) for o in range(1, TP)]

    for kind, n0 in (("i", 0), ("t", HALF)):
        for j in range(3):
            n = f"{kind}{j}"
            total = scatter_sum(jobs[n], 2, rs[n])
            cols = slice(n0 + 128 * j, n0 + 128 * j + 128)
            b["sf"][0, :, cols] = total[:wr]
            b["sf"][1, :, cols] = total[wr:]
    sf_local = local(b["sf"].at[core], gfo.at[core])
    sf_swap = remote(b["sf"].at[other], gfo.at[core], sibling)

    arrived(steps)
    total = b["e3"][x].astype(F32)
    for o in range(1, TP):
        total = total + b["r3"][o - 1].astype(F32)
    b["s4"][...] = total
    s4_local = local(b["s4"].at[core], gao.at[core])
    s4_swap = remote(b["s4"].at[other], gao.at[core], sibling)

    for kind, out_ref in ((3, hout), (5, dxo)):
        for s in range(2):
            for j in range(2):
                from_device(out_ref.at[s, pl.ds(TOKENS * j, TOKENS)], xsem.at[kind, 2 * s + j])
    for s in range(2):
        from_device(mout.at[s], xsem.at[4, s])
    sf_local.wait()
    s4_local.wait()
    arrived([sf_swap, s4_swap])

    for copy in sent:
        copy.wait_send()
    for same, copy in conditional:

        @pl.when(jnp.logical_not(same))
        def _():
            copy.wait_send()

    @pl.when((seg == 0) & (core == 1))
    def _():
        hops[0].wait_send()
        hops[1].wait_send()


def layer(sh, arrays):
    pack, small = selections(sh)
    table = scratch_of(sh)
    names = list(table)
    vmem = pl.BlockSpec(memory_space=pltpu.VMEM)
    outs = [
        jax.ShapeDtypeStruct((2, 128, D), BF16),
        jax.ShapeDtypeStruct((2, 8, D), F32),
        jax.ShapeDtypeStruct((2, 128, D), BF16),
        jax.ShapeDtypeStruct((2, sh.pr, ACOLS), F32),
        jax.ShapeDtypeStruct((2, sh.wrows, D), F32),
    ]
    return pl.pallas_call(
        functools.partial(kernel, sh, names),
        name="layer",
        out_shape=outs,
        in_specs=[vmem] * 7,
        out_specs=[vmem] * len(outs),
        scratch_shapes=[pltpu.VMEM(*table[n]) for n in names]
        + [
            pltpu.SemaphoreType.DMA((180,)),
            pltpu.SemaphoreType.DMA((180,)),
            pltpu.SemaphoreType.DMA((7, 12)),
            pltpu.SemaphoreType.DMA((8,)),
        ],
        compiler_params=pltpu.CompilerParams(
            collective_id=0, has_side_effects=True, vmem_limit_bytes=64 * 2**20 - 2**17
        ),
    )(*arrays, jnp.asarray(pack, BF16), jnp.asarray(small, BF16))


def body(
    sh,
    hidden_in,
    reset,
    w_qkv,
    w_attn_out,
    norm_gains,
    norm_biases,
    memory_tokens,
    w_in,
    w_out,
    grad_hidden,
    grad_memory,
):
    ar, wr = sh.arows, sh.wrows
    small = jnp.concatenate([norm_gains, norm_biases, memory_tokens.reshape(2 * MEM, ar)], 0).T
    small = jnp.pad(small, ((0, 0), (0, SMALL - small.shape[1])))
    by_half = w_qkv.reshape(ar, 3, 2, HALF).transpose(2, 0, 1, 3).reshape(2, ar, 3 * HALF)
    proj = w_attn_out.reshape(ar, 2, HALF).transpose(1, 0, 2)
    pk = jnp.concatenate([by_half, proj, jnp.broadcast_to(small, (2, ar, SMALL))], 2)
    pk = jnp.pad(pk, ((0, 0), (0, sh.pr - ar), (0, 0)))
    up = w_in.reshape(wr, 2, HALF).transpose(1, 0, 2)
    down = w_out.T.reshape(wr, 2, HALF).transpose(1, 0, 2)
    ff = jnp.pad(jnp.concatenate([up, down], 2), ((0, 0), (0, sh.fr - wr), (0, 0)))
    gmem = jnp.pad(grad_memory.astype(F32), ((0, 0), (0, 3), (0, 0)))
    hout, mout, dxo, gao, gfo = layer(sh, (hidden_in, grad_hidden, gmem, pk, ff))

    gq = gao[:, :ar, : 3 * HALF].reshape(2, ar, 3, HALF).transpose(1, 2, 0, 3).reshape(ar, 3 * D)
    gp = gao[:, :ar, 3 * HALF : 4 * HALF].transpose(1, 0, 2).reshape(ar, D)
    gs = (gao[0] + gao[1])[:ar, 4 * HALF : 4 * HALF + 4 + 2 * MEM].T
    gi = gfo[:, :, :HALF].transpose(1, 0, 2).reshape(wr, D)
    gt = gfo[:, :, HALF:].transpose(1, 0, 2).reshape(wr, D).T
    return (
        hout,
        mout[:, :5].astype(BF16),
        dxo.astype(F32),
        gq,
        gp,
        gs[0:2],
        gs[2:4],
        gs[4:].reshape(2, MEM, ar),
        gi,
        gt,
    )


def solution(mesh):
    sh = Shape(mesh.shape["dp"])
    return jax.shard_map(
        functools.partial(body, sh),
        mesh=mesh,
        in_specs=(
            P("dp", "tp", None),
            P("dp"),
            P(("dp", "tp"), None),
            P(("dp", "tp"), None),
            P(None, ("dp", "tp")),
            P(None, ("dp", "tp")),
            P(None, None, ("dp", "tp")),
            P("dp", "tp"),
            P("tp", "dp"),
            P("dp", "tp", None),
            P("dp", "tp", None),
        ),
        out_specs=(
            P("dp", "tp", None),
            P("dp", "tp", None),
            P("dp", "tp", None),
            P(("dp", "tp"), None),
            P(("dp", "tp"), None),
            P(None, ("dp", "tp")),
            P(None, ("dp", "tp")),
            P(None, None, ("dp", "tp")),
            P("dp", "tp"),
            P("tp", "dp"),
        ),
        check_vma=False,
    )
```

time: 1530 us -> 187 us (0.12); the launches traced: 1500 us -> 187 us
  blocking collectives: 650 us -> 0 us
  waiting for transfers between devices: 315 us -> 0 us
  local copies, waits for them, and re-layouts: 236 us -> 11 us
  starting transfers between devices: 183 us -> 0 us
  Pallas kernels: 0 us -> 172 us
  matrix products: 75.3 us -> 0 us
  other arithmetic: 23.5 us -> 2.96 us
  between operations: 16.7 us -> 0.81 us
    unnamed x1 -> x0, blocking collectives: 368 us -> none
    unnamed x77 -> x0, waiting for transfers between devices: 240 us -> none
    all_gather x7 -> x0, blocking collectives: 209 us -> none  [the longest x1 67.8 us: body(): lax.all_gather(memory_tokens, ('dp', 'tp'), axis=2, tiled=True)]
    unnamed x67 -> x0, starting transfers between devices: 176 us -> none
    pallas_call x0 -> x1, Pallas kernels: none -> 172 us  [layer(): pl.pallas_call(functools.partial(kernel, sh, names), name='layer', out_sh...]
    dynamic_update_slice x17 -> x0, local copies, waits for them, and re-layouts: 118 us -> none  [the longest x4 114 us: body(): lax.map(attend_back, (queries, keyvals, logsum, grad_mixed))]
    dot_general x32 -> x0, matrix products: 75.3 us -> none  [the longest x2 8.57 us: forward_step(): jnp.dot(everyone, qkv_full[:, D:], preferred_element_type=jnp.float32)]
    all_gather x5 -> x0, waiting for transfers between devices: 75.1 us -> none  [the longest x1 36.2 us: body(): lax.all_gather(w_in, 'dp', axis=0, tiled=True)]
  transfers between devices with their start and end apart: 78 -> 0, of which waited for: 9 -> 0; matrix products, arithmetic and copies ran while one was open for 30% -> 0% of each run, Pallas kernels for 0% -> 0%
where the time goes in v1:
time: 187 us
  Pallas kernels  172 us (92%)
  local copies, waits for them, and re-layouts  11 us (6%)
  other arithmetic  2.96 us (2%)
    pallas_call x1, Pallas kernels, layer(): pl.pallas_call(functools.partial(kernel, sh, names), name='layer', out_sh...  172 us
    unnamed x32, local copies, waits for them, and re-layouts  4.83 us

profile of v1, /device:TPU:1, one launch (start us, length us, event | category | flops | bytes accessed | tf_op | source)
XLA Modules:
  0.0 186.8 jit_solution(2196562185094320187)
XLA Ops:
  0.7 0.6 copy-done.10
  1.3 0.1 copy.45
  1.4 0.1 copy.46
  1.7 0.6 pad_convert_fusion.refs_2_
  2.4 0.1 copy-done.4
  2.6 0.7 copy-done.8
  3.3 0.7 fusion.6.refs_3_
  4.0 0.1 copy-done.5
  4.1 0.6 fusion.7.refs_4_
  4.8 172.1 %layer.1 = (bf16[2,128,768]{2,1,0:T(8,128)(2,1)}, f32[2,8,768]{2,1,0:T(8,128)}, bf16[2,128,768]{2,1,0:T(8,128)(2,1)}, f32[2,16,1664]{2,1,0:T(8,128)}, f32[2,24,768]{2,1,0:T(8,128)}) custom-call(bf16[2,128,768]{2,1,0:T(8,128)(2,1)} %refs_0_.1, bf16[2,128,768]{2,1,0:T(8,128)(2,1)} %refs_1_.1, f32[2,8,768]{2,1,0:T(8,128)} %pad_convert_fusion.refs_2_, ...), custom_call_target="tpu_custom_call" | custom-call | tf_op jit(solution)/shard_map/layer/pallas_call | solution.py:746
  176.8 0.8 slice.53
  177.7 0.6 copy.54
  178.3 1.3 slice.36
  179.6 0.9 slice.35
  180.7 0.7 reshape.66
  181.4 0.7 copy.56
  182.1 0.6 copy.55
  182.8 0.7 reshape.64
  183.5 0.2 copy-done.3
  183.7 0.6 copy.60
  184.3 0.6 copy.59
  185.0 0.9 convert_element_type.10
  185.9 0.2 copy-done.1
  186.1 0.7 copy.66
  (36 shorter events, 0.7 us)
Async XLA Ops:
  0.6 0.7 copy-start.10
  0.7 0.8 copy-start.11
  0.7 0.9 copy-start.9
  0.7 1.0 copy-start.7
  1.7 0.8 copy-start.4
  2.6 0.7 copy-start.8
  3.3 0.8 copy-start.5
  3.3 0.8 copy-start.6
  176.8 3.7 %copy-start = (f32[2,16,1664]{2,1,0:T(8,128)S(1)}, f32[2,16,1664]{2,1,0:T(8,128)}, u32[]{:S(2)}) copy-start(f32[2,16,1664]{2,1,0:T(8,128)} %get-tuple-element.18) | copy-start | bytes 638980
  182.8 0.9 copy-start.3
  182.8 2.2 %copy-start.2 = (bf16[2,128,768]{2,1,0:T(8,128)(2,1)S(1)}, bf16[2,128,768]{2,1,0:T(8,128)(2,1)}, u32[]{:S(2)}) copy-start(bf16[2,128,768]{2,1,0:T(8,128)(2,1)} %get-tuple-element.17) | copy-start | bytes 1179652
  185.0 1.1 copy-start.1

commit v2 on v1

v2 whole, which is shorter than its diff:
```python
import functools

import jax
import jax.numpy as jnp
import numpy as np
from jax import lax
from jax.experimental import pallas as pl
from jax.experimental.pallas import tpu as pltpu
from jax.sharding import PartitionSpec as P

D = 768
HALF = 384
MEM = 10
TOKENS = 64
OWN = 272
ROWS = 2 * OWN
TP = 4
SMALL = 128
ACOLS = 4 * HALF + SMALL
CUT = 768
WO = 3 * HALF
EPSILON = 1e-05
INV_ROOT_TWO = 0.7071067811865476
INV_ROOT_TWOPI = 0.3989422804014327
EXP_SCALE = 0.125 * 1.4426950408889634
MASKED = -1e30
F32 = jnp.float32
BF16 = jnp.bfloat16
MESH = pl.DeviceIdType.MESH
NN = (((1,), (0,)), ((), ()))
NT = (((1,), (1,)), ((), ()))
TN = (((0,), (0,)), ((), ()))


def dot(a, b, dims=NN):
    return lax.dot_general(a, b, dims, preferred_element_type=F32)


def up16(n):
    return -(-n // 16) * 16


class Shape:
    def __init__(self, dp):
        self.dp = dp
        planes = dp // 2
        self.ny = int(round(planes**0.5))
        self.nz = planes // self.ny
        self.wrows = D // dp
        self.arows = D // (dp * TP)
        self.brows = 2 * self.wrows
        self.pr = up16(self.arows)
        self.pc = -(-self.arows // 8) * 8
        self.fr = up16(self.wrows)


def selections(sh):
    pack = np.zeros((sh.brows, TP * 2 * sh.pc), np.float32)
    for c in range(2):
        for x in range(TP):
            for i in range(sh.arows):
                pack[c * sh.wrows + x * sh.arows + i, (x * 2 + c) * sh.pc + i] = 1
    small = np.zeros((48, SMALL), np.float32)
    for i in range(4):
        small[i, i] = 1
    for kind in range(2):
        for i in range(MEM):
            small[16 + 16 * kind + (i // 5) * 8 + i % 5, 4 + MEM * kind + i] = 1
    return pack, small


def norm_forward(inputs, gain, offset):
    centred = inputs - jnp.mean(inputs, -1, keepdims=True)
    spread = jnp.mean(centred * centred, -1, keepdims=True)
    inverse = lax.rsqrt(spread + EPSILON)
    normed = centred * inverse
    return normed * gain + offset, normed, inverse


def norm_backward(upstream, normed, inverse, gain):
    scaled = upstream * gain
    first_mean = jnp.mean(scaled, -1, keepdims=True)
    second_mean = jnp.mean(scaled * normed, -1, keepdims=True)
    return inverse * (scaled - first_mean - normed * second_mean)


def column_sum(a):
    return jnp.sum(a, 0, keepdims=True)


SCRATCH = {}


def scratch_of(sh):
    nz, ny, br = sh.nz, sh.ny, sh.brows
    s = {
        "p1": ((2, sh.pr, ACOLS), BF16),
        "p2": ((TP, 2 * sh.pc, ACOLS), BF16),
        "f1": ((2, sh.fr, D), BF16),
        "wa": ((nz, ny, br, ACOLS), BF16),
        "wf": ((TP, nz, ny, br, D), BF16),
        "wo": ((2, nz, ny, br, HALF), BF16),
        "par": ((8, D), F32),
        "x": ((ROWS, D), BF16),
        "gyt": ((TP * TOKENS, D), BF16),
        "gm": ((2, 8, D), F32),
        "qkv": ((9, ROWS, 128), BF16),
        "pt": ((6, ROWS, ROWS), BF16),
        "ot": ((3, 128, ROWS), BF16),
        "oc": ((ROWS, HALF), BF16),
        "oown": ((2, OWN, HALF), BF16),
        "h1": ((OWN, D), F32),
        "n1": ((OWN, D), F32),
        "inv1": ((OWN, 1), F32),
        "h1b": ((ROWS, D), BF16),
        "gl": ((2, ROWS, D), BF16),
        "sl": ((2, ROWS, D), BF16),
        "fs": ((OWN, D), BF16),
        "fr": ((OWN, D), BF16),
        "n2": ((OWN, D), F32),
        "yb": ((OWN, D), BF16),
        "mo": ((2, 8, D), F32),
        "hop": ((16, D), BF16),
        "hopin": ((16, D), BF16),
        "es": ((16, D), F32),
        "er": ((16, D), F32),
        "dz": ((OWN, D), F32),
        "dfb": ((ROWS, D), BF16),
        "du": ((2, ROWS, D), BF16),
        "dhs": ((OWN, D), BF16),
        "dhr": ((OWN, D), BF16),
        "dr": ((OWN, D), F32),
        "dab": ((ROWS, D), BF16),
        "doc": ((3, ROWS, 128), BF16),
        "dqkv": ((9, ROWS, 128), BF16),
        "ga": ((nz, ny, br, ACOLS), BF16),
        "gi": ((TP, nz, ny, br, HALF), BF16),
        "gt": ((TP, nz, ny, br, HALF), BF16),
        "gos": ((D // 2 // br if nz > 1 else 1, br if nz > 1 else HALF, HALF), BF16),
        "dxs": ((OWN, D), BF16),
        "dxr": ((OWN, D), BF16),
        "dxb": ((TP * TOKENS, D), BF16),
        "sg": ((48, D), F32),
        "e3": ((TP, 2 * sh.pc, ACOLS), BF16),
        "r3": ((TP - 1, 2 * sh.pc, ACOLS), BF16),
        "s4": ((2, sh.pc, ACOLS), F32),
        "sf": ((2, sh.wrows, D), F32),
    }
    if nz > 1:
        s["gos"] = ((nz // 2, ny, br, HALF), BF16)
    else:
        s["gos"] = ((1, 1, HALF, HALF), BF16)
    sizes = {"x": TP, "z": nz, "y": ny}
    for name, order, cols, axes in scatter_jobs():
        left = [a for a in axes]
        for step, axis in enumerate(order):
            left = [a for a in left if a != axis]
            dims = tuple(sizes[a] for a in left)
            s[f"r{step}_{name}"] = ((max(1, sizes[axis] - 1),) + dims + (br, cols.stop - cols.start), BF16)
            if step < len(order) - 1:
                s[f"s{step}_{name}"] = (dims + (br, cols.stop - cols.start), BF16)
    return s


def scatter_jobs():
    orders = [("z", "y", "x"), ("x", "z", "y"), ("y", "x", "z")]
    jobs = []
    for kind in ("t", "i"):
        for j in range(3):
            jobs.append((f"{kind}{j}", orders[j], slice(128 * j, 128 * j + 128), ("x", "z", "y")))
    zy, yz = ("z", "y"), ("y", "z")
    jobs.append(("aw", yz, slice(WO, WO + HALF), zy))
    jobs.append(("a0", zy, slice(0, HALF), zy))
    jobs.append(("a1", yz, slice(HALF, 2 * HALF), zy))
    jobs.append(("a2", zy, slice(2 * HALF, 2 * HALF + 256), zy))
    jobs.append(("a3", yz, slice(2 * HALF + 256, 3 * HALF), zy))
    jobs.append(("as", yz, slice(4 * HALF, ACOLS), zy))
    return jobs


def gather_jobs():
    orders = [("x", "y", "z"), ("y", "z", "x"), ("z", "x", "y")]
    jobs = [(f"f{j}", orders[j], slice(256 * j, 256 * j + 256), ("x", "z", "y")) for j in range(3)]
    jobs.append(("a0", ("y", "z"), slice(0, CUT), ("z", "y")))
    jobs.append(("a1", ("z", "y"), slice(CUT, ACOLS), ("z", "y")))
    return jobs


WEIGHTS = {"f": "wf", "a": "wa"}
GRADS = {"t": "gt", "i": "gi", "a": "ga"}


def kernel(sh, names, *refs):
    xin, gin, gmem, pk, ff, packsel, smallsel = refs[:7]
    hout, mout, dxo, gao, gfo = refs[7:12]
    b = dict(zip(names, refs[12 : 12 + len(names)]))
    ssem, rsem, xsem, lsem = refs[12 + len(names) :]
    nz, ny, br, wr, pr = sh.nz, sh.ny, sh.brows, sh.wrows, sh.pr

    dp = lax.axis_index("dp")
    x = lax.axis_index("tp")
    core = dp % 2
    y = (dp // 2) % ny
    z = dp // (2 * ny)
    other = 1 - core
    chain = x // 2
    seg = jnp.where((x == 1) | (x == 2), 1, 0)
    at = {"x": x, "y": y, "z": z}
    size = {"x": TP, "y": ny, "z": nz}

    def device(x_=x, y_=y, z_=z, c_=core):
        return ((z_ * ny + y_) * 2 + c_, x_)

    def moved(axis, offset, core_=core):
        there = dict(at)
        there[axis] = (at[axis] + offset) % size[axis]
        return device(there["x"], there["y"], there["z"], core_)

    sibling = device(c_=other)
    counts = {"s": 0, "r": 0}
    sent = []

    def remote(src, dst, to):
        copy = pltpu.make_async_remote_copy(
            src_ref=src,
            dst_ref=dst,
            send_sem=ssem.at[counts["s"]],
            recv_sem=rsem.at[counts["r"]],
            device_id=to,
            device_id_type=MESH,
        )
        counts["s"] += 1
        counts["r"] += 1
        copy.start()
        sent.append(copy)
        return copy

    def arrived(copies):
        for copy in copies:
            copy.wait_recv()

    locals_ = [0]

    def local(src, dst):
        copy = pltpu.make_async_copy(src, dst, lsem.at[locals_[0]])
        locals_[0] += 1
        copy.start()
        return copy

    barrier = pltpu.get_barrier_semaphore()
    peers = [sibling]
    for o in range(1, TP):
        peers += [moved("x", o), moved("x", o, other)]
    for axis in ("y", "z"):
        for o in range(1, size[axis]):
            peers.append(moved(axis, o))
    for peer in peers:
        pl.semaphore_signal(barrier, inc=1, device_id=peer, device_id_type=MESH)
    pl.semaphore_wait(barrier, len(peers))

    pk_local = local(pk.at[core], b["p1"].at[core])
    ff_local = local(ff.at[core], b["f1"].at[core])
    pk_swap = remote(pk.at[other], b["p1"].at[core], sibling)
    ff_swap = remote(ff.at[other], b["f1"].at[core], sibling)

    conditional = []

    def to_device(src, dst, place, here, kind, send_slot):
        copy = pltpu.make_async_remote_copy(
            src_ref=src,
            dst_ref=dst,
            send_sem=xsem.at[kind, 8 + send_slot],
            recv_sem=here,
            device_id=device(x_=place[0], c_=place[1]),
            device_id_type=MESH,
        )
        same = (place[0] == x) & (place[1] == core)

        @pl.when(same)
        def _():
            pltpu.make_async_copy(src, dst, here).start()

        @pl.when(jnp.logical_not(same))
        def _():
            copy.start()

        conditional.append((same, copy))

    def from_device(dst, kind, slot):
        pltpu.make_async_copy(dst, dst, xsem.at[kind, slot]).wait()

    def chip_of(k, s):
        return s + k * (3 - 2 * s)

    def send_rows():
        for s in range(2):
            for j in range(2):
                to_device(
                    xin.at[s, pl.ds(TOKENS * j, TOKENS)],
                    b["x"].at[pl.ds(pl.multiple_of(OWN * j + TOKENS * x, 16), TOKENS)],
                    (chip_of(core, s), j),
                    xsem.at[0, x],
                    0,
                    2 * s + j,
                )

    def send_upstream():
        for s in range(2):
            for j in range(2):
                to_device(
                    gin.at[s, pl.ds(TOKENS * j, TOKENS)],
                    b["gyt"].at[pl.ds(pl.multiple_of(TOKENS * x, 16), TOKENS)],
                    (chip_of(core, s), j),
                    xsem.at[1, x],
                    1,
                    2 * s + j,
                )
            to_device(
                gmem.at[s], b["gm"].at[x % 2], (chip_of(core, s), x // 2), xsem.at[2, x % 2], 2, s
            )

    def part_of(job, step, place, half=None):
        name, order, cols, axes = job
        fixed = {a: at[a] for a in order[step:]}
        fixed[order[step]] = place
        where = []
        for a in axes:
            if a in fixed:
                where.append(fixed[a])
            elif half is not None:
                where.append(pl.ds(half * (size[a] // 2), size[a] // 2))
                half = None
            else:
                where.append(slice(None))
        return b[WEIGHTS[name[0]]].at[tuple(where) + (slice(None), cols)]

    def gather_start(name, step):
        job = gathers[name]
        axis = job[1][step]
        n = size[axis]
        own = part_of(job, step, at[axis])
        free = [a for a in job[3] if a not in job[1][step:]]
        relay = n == 4 and len(free) > 0 and size[free[0]] % 2 == 0
        state = {"step": step, "relay": relay}
        if relay:
            state["right"] = remote(own, own, moved(axis, 1))
            state["left"] = remote(own, own, moved(axis, n - 1))
        else:
            state["all"] = [remote(own, own, moved(axis, o)) for o in range(1, n)]
        flying[name] = state

    def gather_pass(name):
        job, state = gathers[name], flying[name]
        if not state["relay"]:
            return
        axis = job[1][state["step"]]
        n = size[axis]
        state["all"] = []
        for kind, back, onward, half in (("right", n - 1, 1, 0), ("left", 1, n - 1, 1)):
            arrived([state[kind]])
            piece = part_of(job, state["step"], (at[axis] + back) % n, half)
            state["all"].append(remote(piece, piece, moved(axis, onward)))

    def gather_done(name):
        arrived(flying[name]["all"])

    gathers = {j[0]: j for j in gather_jobs()}
    flying = {}

    pk_local.wait()
    arrived([pk_swap])
    two = [b["p1"][c].astype(F32)[: sh.pc] for c in range(2)]
    b["p2"][x] = jnp.concatenate(two, 0).astype(BF16)
    mine = b["p2"].at[x]
    steps = [remote(mine, mine, moved("x", o)) for o in range(1, TP)]
    ff_local.wait()
    arrived([ff_swap])
    two = [b["f1"][c].astype(F32)[:wr] for c in range(2)]
    b["wf"][x, z, y] = jnp.concatenate(two, 0).astype(BF16)
    for n in ("f1", "f2", "f0"):
        gather_start(n, 0)
    send_rows()
    arrived(steps)
    b["wa"][z, y] = dot(packsel[...], b["p2"][...].reshape(TP * 2 * sh.pc, ACOLS)).astype(BF16)
    for n in ("a0", "a1"):
        gather_start(n, 0)
    for n in ("f1", "f2", "f0"):
        gather_done(n)
        gather_start(n, 1)
    for n in ("a0", "a1"):
        gather_done(n)
        gather_start(n, 1)
    for n in ("f1", "f2", "f0"):
        gather_pass(n)
    gather_done("f1")
    gather_start("f1", 2)
    for n in ("a0", "a1"):
        gather_pass(n)
    for n in ("f2", "f0"):
        gather_done(n)
        gather_start(n, 2)

    for i in range(TP):
        from_device(b["x"].at[pl.ds(pl.multiple_of(OWN * core + TOKENS * i, 16), TOKENS)], 0, i)
    half = b["x"].at[pl.ds(pl.multiple_of(OWN * core, 16), TP * TOKENS)]
    x_swap = remote(half, half, sibling)
    gather_pass("f1")
    for n in ("a0", "a1"):
        gather_done(n)
    wo_cols = slice(WO, WO + HALF)
    wo_local = local(b["wa"].at[:, :, :, wo_cols], b["wo"].at[core])
    wo_swap = remote(b["wa"].at[:, :, :, wo_cols], b["wo"].at[core], sibling)
    send_upstream()

    def attention_weight():
        return b["wa"][:, :, :, :WO].reshape(D, WO)

    small = b["wa"][:, :, :, 4 * HALF :].reshape(D, SMALL)
    chosen = dot(smallsel[...], small, NT)
    b["par"][...] = chosen[0:8]
    b["x"][OWN + 256 : OWN + 272] = chosen[32:48].astype(BF16)

    @pl.when(seg == 0)
    def _():
        b["x"][256:272] = chosen[16:32].astype(BF16)

    @pl.when(seg == 1)
    def _():
        b["x"][256:272] = jnp.zeros((16, D), BF16)

    gains = [b["par"][i : i + 1] for i in range(2)]
    biases = [b["par"][2 + i : 3 + i] for i in range(2)]
    arrived([x_swap])

    hop_to = jnp.where(x == 0, 1, 2)
    hops = []
    for j in range(2):
        hops.append(
            pltpu.make_async_remote_copy(
                src_ref=b["hop"],
                dst_ref=b["hopin"],
                send_sem=xsem.at[6, j],
                recv_sem=xsem.at[6, 2],
                device_id=device(x_=hop_to, c_=j),
                device_id_type=MESH,
            )
        )

    own_rows = pl.ds(pl.multiple_of(OWN * core, 16), OWN)
    other_rows = pl.ds(pl.multiple_of(OWN * other, 16), OWN)

    out = dot(b["x"][...], attention_weight()).astype(BF16)
    for i in range(9):
        b["qkv"][i] = out[:, 128 * i : 128 * i + 128]

    def head_masks(hh):
        lane = lax.broadcasted_iota(jnp.int32, (ROWS, 128), 1)
        row = lax.broadcasted_iota(jnp.int32, (ROWS, 128), 0)
        inside = (lane // 64) == hh
        spare = lane == 64 * (1 - hh)
        memory = ((row >= 256) & (row < 272)) | (row >= OWN + 256)
        invalid = memory & (row % 8 >= 5)
        return inside, spare, invalid

    def forward_pair(p):
        qp, kp, vp = (b["qkv"][3 * p + i] for i in range(3))
        vt = vp.T
        for hh in range(2):
            inside, spare, invalid = head_masks(hh)
            zero = jnp.zeros_like(kp)
            kmask = jnp.where(spare & invalid, jnp.full_like(kp, MASKED), zero)
            km = jnp.where(inside, kp, kmask)
            qm = jnp.where(inside, qp, jnp.where(spare, jnp.ones_like(qp), zero))
            scores = dot(km, qm, NT)
            peak = jnp.max(scores, 0, keepdims=True)
            raised = jnp.exp2((scores - peak) * EXP_SCALE)
            total = jnp.sum(raised, 0, keepdims=True)
            probs = (raised * (1.0 / total)).astype(BF16)
            b["pt"][2 * p + hh] = probs
            b["ot"][p, 64 * hh : 64 * hh + 64] = dot(vt[64 * hh : 64 * hh + 64], probs).astype(BF16)
        b["oc"][:, 128 * p : 128 * p + 128] = b["ot"][p].T

    @pl.when(seg == 0)
    def _():
        forward_pair(0)
        forward_pair(1)

    for n in ("f2", "f0"):
        gather_pass(n)

    @pl.when(seg == 0)
    def _():
        forward_pair(2)

    @pl.when(seg == 1)
    def _():
        hops[0].wait_recv()
        b["x"][256:272] = b["hopin"][...]
        rows = dot(b["hopin"][...], attention_weight()).astype(BF16)
        for i in range(9):
            b["qkv"][i, 256:272] = rows[:, 128 * i : 128 * i + 128]
        for p in range(3):
            forward_pair(p)

    o_local = local(b["oc"].at[own_rows], b["oown"].at[core])
    o_swap = remote(b["oc"].at[other_rows], b["oown"].at[core], sibling)
    wo_local.wait()
    arrived([wo_swap])
    o_local.wait()
    arrived([o_swap])
    halves = []
    for h in range(2):
        w = b["wo"][h].reshape(D, HALF)
        halves.append(dot(b["oown"][0], w[:HALF]) + dot(b["oown"][1], w[HALF:]))
    attended = jnp.concatenate(halves, 1)
    h1, n1, inv1 = norm_forward(b["x"][own_rows].astype(F32) + attended, gains[0], biases[0])
    b["h1"][...] = h1
    b["n1"][...] = n1
    b["inv1"][...] = inv1
    b["h1b"][own_rows] = h1.astype(BF16)
    h_swap = remote(b["h1b"].at[own_rows], b["h1b"].at[own_rows], sibling)
    for n in ("f1", "f2", "f0"):
        gather_done(n)
    arrived([h_swap])

    def feed_weight(t, kind):
        cols = [256 * j + 128 * kind for j in range(3)]
        blocks = [b["wf"][2 * t + i, :, :, :, c : c + 128].reshape(D, 128) for i in range(2) for c in cols]
        return jnp.concatenate(blocks, 1)

    def up_weight(t):
        return feed_weight(t, 0)

    def down_weight(t):
        return feed_weight(t, 1)

    def activate(units):
        erf = 0.5 * (1.0 + lax.erf(units * INV_ROOT_TWO))
        return (units * erf).astype(BF16), erf

    early = pltpu.make_async_remote_copy(
        src_ref=b["es"],
        dst_ref=b["er"],
        send_sem=xsem.at[6, 3],
        recv_sem=xsem.at[6, 4],
        device_id=sibling,
        device_id_type=MESH,
    )
    row16 = lax.broadcasted_iota(jnp.int32, (16, D), 0)

    @pl.when(seg == 0)
    def _():
        rows = b["h1b"][OWN + 256 : OWN + 272]
        part = sum(dot(activate(dot(rows, up_weight(t)))[0], down_weight(t), NT) for t in range(2))

        @pl.when(core == 0)
        def _():
            b["es"][...] = part
            early.start()

        @pl.when(core == 1)
        def _():
            early.wait_recv()
            whole = b["h1"][256:272] + part + b["er"][...]
            written = norm_forward(whole, gains[1], biases[1])[0]
            b["hop"][...] = jnp.where(row16 % 8 < 5, written, 0.0).astype(BF16)
            hops[0].start()
            hops[1].start()

    for t in range(2):
        units = dot(b["h1b"][...], up_weight(t))
        active, erf = activate(units)
        b["gl"][t] = active
        b["sl"][t] = (erf + units * jnp.exp(-0.5 * units * units) * INV_ROOT_TWOPI).astype(BF16)

    def partial_down(rows):
        return sum(dot(b["gl"][t, rows], down_weight(t), NT) for t in range(2))

    b["fs"][...] = partial_down(other_rows).astype(BF16)
    f_swap = remote(b["fs"], b["fr"], sibling)
    branch = partial_down(own_rows)
    arrived([f_swap])
    out, n2, inv2 = norm_forward(b["h1"][...] + branch + b["fr"][...].astype(F32), gains[1], biases[1])
    low = out.astype(BF16)
    b["yb"][...] = low
    b["mo"][...] = low[256:272].astype(F32).reshape(2, 8, D)
    for i in range(TP):
        to_device(
            b["yb"].at[pl.ds(TOKENS * i, TOKENS)],
            hout.at[seg, pl.ds(pl.multiple_of(TOKENS * core, 16), TOKENS)],
            (i, chain),
            xsem.at[3, 2 * seg + core],
            3,
            i,
        )
    for i in range(2):
        to_device(b["mo"].at[i], mout.at[seg], (2 * core + i, chain), xsem.at[4, seg], 4, i)

    for i in range(TP):
        from_device(b["gyt"].at[pl.ds(TOKENS * i, TOKENS)], 1, i)
    for i in range(2):
        from_device(b["gm"].at[i], 2, i)
    upstream = jnp.concatenate([b["gyt"][...].astype(F32), b["gm"][...].reshape(16, D)], 0)
    b["sg"][...] = jnp.zeros((48, D), F32)
    b["sg"][1:2] = column_sum(upstream * n2)
    b["sg"][3:4] = column_sum(upstream)
    dz = norm_backward(upstream, n2, inv2, gains[1])
    b["dz"][...] = dz
    b["dfb"][own_rows] = dz.astype(BF16)
    df_swap = remote(b["dfb"].at[own_rows], b["dfb"].at[own_rows], sibling)
    arrived([df_swap])

    for t in range(2):
        b["du"][t] = (dot(b["dfb"][...], down_weight(t)) * b["sl"][t].astype(F32)).astype(BF16)

    def partial_up(rows):
        return sum(dot(b["du"][t, rows], up_weight(t), NT) for t in range(2))

    def weight_grad(name, left, right):
        for t in range(2):
            part = dot(left, b[right][t], TN).astype(BF16)
            for i in range(2):
                b[name][2 * t + i] = part[:, HALF * i : HALF * (i + 1)].reshape(nz, ny, br, HALF)

    b["dhs"][...] = partial_up(other_rows).astype(BF16)
    dh_swap = remote(b["dhs"], b["dhr"], sibling)
    b["dz"][...] = b["dz"][...] + partial_up(own_rows)
    weight_grad("gt", b["dfb"][...], "gl")

    def pick(axes, axis, place):
        return tuple(place if a == axis else slice(None) for a in axes)

    scatters = {j[0]: j for j in scatter_jobs()}
    rs = {}

    def scatter_send(name, step):
        _, order, cols, axes = scatters[name]
        axis = order[step]
        left = [a for a in axes if a not in order[:step]]
        if step == 0:
            source = b[GRADS[name[0]]]
            tail = (slice(None), cols)
        else:
            source = b[f"s{step - 1}_{name}"]
            tail = ()
        copies = []
        for o in range(1, size[axis]):
            there = (at[axis] + o) % size[axis]
            copies.append(
                remote(source.at[pick(left, axis, there) + tail], b[f"r{step}_{name}"].at[o - 1], moved(axis, o))
            )
        rs[name] = copies

    def scatter_sum(name, step):
        _, order, cols, axes = scatters[name]
        axis = order[step]
        left = [a for a in axes if a not in order[:step]]
        arrived(rs[name])
        if step == 0:
            mine = b[GRADS[name[0]]][pick(left, axis, at[axis]) + (slice(None), cols)]
        else:
            mine = b[f"s{step - 1}_{name}"][pick(left, axis, at[axis])]
        total = mine.astype(F32)
        for o in range(1, size[axis]):
            total = total + b[f"r{step}_{name}"][o - 1].astype(F32)
        if step < len(order) - 1:
            b[f"s{step}_{name}"][...] = total.astype(BF16)
        return total

    def scatter_on(names, step):
        for n in names:
            scatter_sum(n, step)
            scatter_send(n, step + 1)

    down_names, up_names = ("t0", "t1", "t2"), ("i0", "i1", "i2")
    for n in down_names:
        scatter_send(n, 0)
    weight_grad("gi", b["h1b"][...], "du")
    for n in up_names:
        scatter_send(n, 0)
    arrived([dh_swap])
    into_first = b["dz"][...] + b["dhr"][...].astype(F32)
    b["sg"][0:1] = column_sum(into_first * b["n1"][...])
    b["sg"][2:3] = column_sum(into_first)
    dr = norm_backward(into_first, b["n1"][...], b["inv1"][...], gains[0])
    b["dr"][...] = dr
    b["dab"][own_rows] = dr.astype(BF16)
    da_swap = remote(b["dab"].at[own_rows], b["dab"].at[own_rows], sibling)
    arrived([da_swap])

    def head_rows(ref, c):
        if nz > 1:
            return ref.at[pl.ds(c * (nz // 2), nz // 2)]
        return ref.at[:, :, pl.ds(pl.multiple_of(c * HALF, 16), HALF)]

    grad_mixed = 0.0
    for h in range(2):
        w = head_rows(b["wo"].at[h], core)[...].reshape(HALF, HALF)
        grad_mixed = grad_mixed + dot(b["dab"][:, HALF * h : HALF * (h + 1)], w, NT)
    for p in range(3):
        b["doc"][p] = grad_mixed[:, 128 * p : 128 * p + 128].astype(BF16)

    mixed_t = b["ot"][...].reshape(HALF, ROWS)

    def proj_grad(h):
        cols = pl.ds(pl.multiple_of(HALF * h, 128), HALF)
        return dot(mixed_t, b["dab"][:, cols]).astype(BF16).reshape(b["gos"].shape)

    def wo_part(c):
        return head_rows(b["ga"].at[:, :, :, wo_cols], c)

    b["gos"][...] = proj_grad(other)
    go_swap = remote(b["gos"], wo_part(core), sibling)
    wo_part(core)[...] = proj_grad(core)
    scatter_on(down_names, 0)
    arrived([go_swap])
    scatter_send("aw", 0)

    def backward_pair(p):
        qp, kp, vp = (b["qkv"][3 * p + i] for i in range(3))
        dop = b["doc"][p]
        kt = kp.T
        dv = dk = 0.0
        dq = []
        for hh in range(2):
            inside, _, _ = head_masks(hh)
            zero = jnp.zeros_like(kp)
            grad_probs = dot(jnp.where(inside, vp, zero), dop, NT)
            low_probs = b["pt"][2 * p + hh]
            probs = low_probs.astype(F32)
            row_term = jnp.sum(probs * grad_probs, 0, keepdims=True)
            ds = (probs * (grad_probs - row_term)).astype(BF16)
            dv = dv + dot(low_probs, jnp.where(inside, dop, zero))
            dk = dk + dot(ds, jnp.where(inside, qp, zero))
            dq.append(dot(kt[64 * hh : 64 * hh + 64], ds))
        b["dqkv"][3 * p] = (jnp.concatenate(dq, 0) * 0.125).T.astype(BF16)
        b["dqkv"][3 * p + 1] = (dk * 0.125).astype(BF16)
        b["dqkv"][3 * p + 2] = dv.astype(BF16)

    def joined(rows, wanted):
        return jnp.concatenate([b["dqkv"][i, rows] for i in wanted], 1)

    def attention_grad(p):
        part = dot(b["x"][...], joined(slice(None), range(3 * p, 3 * p + 3)), TN).astype(BF16)
        b["ga"][:, :, :, HALF * p : HALF * (p + 1)] = part.reshape(nz, ny, br, HALF)

    backward_pair(0)
    attention_grad(0)
    scatter_send("a0", 0)
    scatter_on(up_names, 0)
    backward_pair(1)
    attention_grad(1)
    scatter_send("a1", 0)
    scatter_on(down_names, 1)
    backward_pair(2)
    attention_grad(2)
    scatter_send("a2", 0)
    scatter_send("a3", 0)

    def partial_input(rows):
        return dot(joined(rows, range(9)), attention_weight(), NT)

    b["dxs"][...] = partial_input(other_rows).astype(BF16)
    dx_swap = remote(b["dxs"], b["dxr"], sibling)
    dx = partial_input(own_rows) + b["dr"][...]
    arrived([dx_swap])
    dx = dx + b["dxr"][...].astype(F32)
    b["dxb"][...] = dx[:256].astype(BF16)
    for i in range(TP):
        to_device(
            b["dxb"].at[pl.ds(TOKENS * i, TOKENS)],
            dxo.at[seg, pl.ds(pl.multiple_of(TOKENS * core, 16), TOKENS)],
            (i, chain),
            xsem.at[5, 2 * seg + core],
            5,
            i,
        )

    @pl.when((core == 0) & (seg == 0))
    def _():
        b["sg"][16:32] = dx[256:272]

    @pl.when(core == 1)
    def _():
        b["sg"][32:48] = dx[256:272]

    small_grads = dot(b["sg"][...].astype(BF16), smallsel[...], TN).astype(BF16)
    b["ga"][:, :, :, 4 * HALF :] = small_grads.reshape(nz, ny, br, SMALL)
    scatter_send("as", 0)
    attention_names = ("aw", "a0", "a1", "a2", "a3", "as")
    scatter_on(up_names, 1)
    scatter_on(attention_names, 0)

    def last_rows(names, first_col):
        for j, n in enumerate(names):
            total = scatter_sum(n, 2)
            cols = slice(first_col + 128 * j, first_col + 128 * j + 128)
            b["sf"][0, :, cols] = total[:wr]
            b["sf"][1, :, cols] = total[wr:]

    last_rows(down_names, HALF)
    for n in attention_names:
        cols = scatters[n][2]
        spread = dot(packsel[...], scatter_sum(n, 1).astype(BF16), TN).astype(BF16)
        b["e3"][:, :, cols] = spread.reshape(TP, 2 * sh.pc, cols.stop - cols.start)
    steps = [remote(b["e3"].at[(x + o) % TP], b["r3"].at[o - 1], moved("x", o)) for o in range(1, TP)]
    last_rows(up_names, 0)
    sf_local = local(b["sf"].at[core], gfo.at[core])
    sf_swap = remote(b["sf"].at[other], gfo.at[core], sibling)

    arrived(steps)
    total = b["e3"][x].astype(F32)
    for o in range(1, TP):
        total = total + b["r3"][o - 1].astype(F32)
    b["s4"][...] = total.reshape(2, sh.pc, ACOLS)
    s4_local = local(b["s4"].at[core], gao.at[core])
    s4_swap = remote(b["s4"].at[other], gao.at[core], sibling)

    for kind, out_ref in ((3, hout), (5, dxo)):
        for s in range(2):
            for j in range(2):
                from_device(out_ref.at[s, pl.ds(TOKENS * j, TOKENS)], kind, 2 * s + j)
    for s in range(2):
        from_device(mout.at[s], 4, s)
    sf_local.wait()
    s4_local.wait()
    arrived([sf_swap, s4_swap])

    for copy in sent:
        copy.wait_send()
    for same, copy in conditional:

        @pl.when(jnp.logical_not(same))
        def _():
            copy.wait_send()

    @pl.when((seg == 0) & (core == 1))
    def _():
        hops[0].wait_send()
        hops[1].wait_send()

    @pl.when((seg == 0) & (core == 0))
    def _():
        early.wait_send()


def layer(sh, arrays):
    pack, small = selections(sh)
    table = scratch_of(sh)
    names = list(table)
    vmem = pl.BlockSpec(memory_space=pltpu.VMEM)
    outs = [
        jax.ShapeDtypeStruct((2, 128, D), BF16),
        jax.ShapeDtypeStruct((2, 8, D), F32),
        jax.ShapeDtypeStruct((2, 128, D), BF16),
        jax.ShapeDtypeStruct((2, sh.pc, ACOLS), F32),
        jax.ShapeDtypeStruct((2, sh.wrows, D), F32),
    ]
    return pl.pallas_call(
        functools.partial(kernel, sh, names),
        name="layer",
        out_shape=outs,
        in_specs=[vmem] * 7,
        out_specs=[vmem] * len(outs),
        scratch_shapes=[pltpu.VMEM(*table[n]) for n in names]
        + [
            pltpu.SemaphoreType.DMA((200,)),
            pltpu.SemaphoreType.DMA((200,)),
            pltpu.SemaphoreType.DMA((7, 12)),
            pltpu.SemaphoreType.DMA((8,)),
        ],
        compiler_params=pltpu.CompilerParams(
            collective_id=0, has_side_effects=True, vmem_limit_bytes=64 * 2**20 - 2**17
        ),
    )(*arrays, jnp.asarray(pack, BF16), jnp.asarray(small, BF16))


def unpack_kernel(sh, hout, mout, dxo, gao, gfo, *outs):
    hidden, memory, grad_in, gq, gp, gains, biases, tokens, gi, gt = outs
    ar = sh.arows
    hidden[...] = hout[...]
    memory[...] = mout[...][:, :5].astype(BF16)
    grad_in[...] = dxo[...].astype(F32)
    for h in range(2):
        for p in range(3):
            for i in range(3):
                to = D * i + HALF * h + 128 * p
                first = HALF * p + 128 * i
                gq[:, to : to + 128] = gao[h, :ar, first : first + 128]
        gp[:, HALF * h : HALF * (h + 1)] = gao[h, :ar, WO : WO + HALF]
        gi[:, HALF * h : HALF * (h + 1)] = gfo[h, :, :HALF]
        gt[HALF * h : HALF * (h + 1), :] = gfo[h, :, HALF:].T
    small = (gao[0, :, 4 * HALF :] + gao[1, :, 4 * HALF :]).T[:, :ar]
    gains[...] = small[0:2]
    biases[...] = small[2:4]
    for kind in range(2):
        tokens[kind] = small[4 + MEM * kind : 4 + MEM * (kind + 1)]


def unpack(sh, *arrays):
    ar, wr = sh.arows, sh.wrows
    shapes = [
        ((2, 128, D), BF16),
        ((2, 5, D), BF16),
        ((2, 128, D), F32),
        ((ar, 3 * D), F32),
        ((ar, D), F32),
        ((2, ar), F32),
        ((2, ar), F32),
        ((2, MEM, ar), F32),
        ((wr, D), F32),
        ((D, wr), F32),
    ]
    vmem = pl.BlockSpec(memory_space=pltpu.VMEM)
    return pl.pallas_call(
        functools.partial(unpack_kernel, sh),
        name="unpack",
        out_shape=[jax.ShapeDtypeStruct(*one) for one in shapes],
        in_specs=[vmem] * 5,
        out_specs=[vmem] * len(shapes),
        compiler_params=pltpu.CompilerParams(vmem_limit_bytes=32 * 2**20),
    )(*arrays)


def body(
    sh,
    hidden_in,
    reset,
    w_qkv,
    w_attn_out,
    norm_gains,
    norm_biases,
    memory_tokens,
    w_in,
    w_out,
    grad_hidden,
    grad_memory,
):
    ar, wr = sh.arows, sh.wrows
    small = jnp.concatenate([norm_gains, norm_biases, memory_tokens.reshape(2 * MEM, ar)], 0).T
    small = jnp.pad(small, ((0, 0), (0, SMALL - small.shape[1])))
    by_half = w_qkv.reshape(ar, 3, 2, 3, 128).transpose(2, 0, 3, 1, 4).reshape(2, ar, 3 * HALF)
    proj = w_attn_out.reshape(ar, 2, HALF).transpose(1, 0, 2)
    pk = jnp.concatenate([by_half, proj, jnp.broadcast_to(small, (2, ar, SMALL))], 2)
    pk = jnp.pad(pk, ((0, 0), (0, sh.pr - ar), (0, 0)))
    both = jnp.stack([w_in.reshape(wr, 2, 3, 128), w_out.T.reshape(wr, 2, 3, 128)], 3)
    ff = both.transpose(1, 0, 2, 3, 4).reshape(2, wr, D)
    ff = jnp.pad(ff, ((0, 0), (0, sh.fr - wr), (0, 0)))
    gmem = jnp.pad(grad_memory.astype(F32), ((0, 0), (0, 3), (0, 0)))
    hout, mout, dxo, gao, gfo = layer(sh, (hidden_in, grad_hidden, gmem, pk, ff))

    return unpack(sh, hout, mout, dxo, gao, gfo)


def solution(mesh):
    sh = Shape(mesh.shape["dp"])
    return jax.shard_map(
        functools.partial(body, sh),
        mesh=mesh,
        in_specs=(
            P("dp", "tp", None),
            P("dp"),
            P(("dp", "tp"), None),
            P(("dp", "tp"), None),
            P(None, ("dp", "tp")),
            P(None, ("dp", "tp")),
            P(None, None, ("dp", "tp")),
            P("dp", "tp"),
            P("tp", "dp"),
            P("dp", "tp", None),
            P("dp", "tp", None),
        ),
        out_specs=(
            P("dp", "tp", None),
            P("dp", "tp", None),
            P("dp", "tp", None),
            P(("dp", "tp"), None),
            P(("dp", "tp"), None),
            P(None, ("dp", "tp")),
            P(None, ("dp", "tp")),
            P(None, None, ("dp", "tp")),
            P("dp", "tp"),
            P("tp", "dp"),
        ),
        check_vma=False,
    )
```

time: 187 us -> 149 us (0.80)
  Pallas kernels: 172 us -> 136 us
    pallas_call x1, Pallas kernels: 172 us -> 135 us  [layer(): pl.pallas_call(functools.partial(kernel, sh, names), name='layer', out_sh...]
    slice x6 -> x0, local copies, waits for them, and re-layouts: 3.25 us -> none  [the longest x1 1.35 us: body(): gp = gao[:, :ar, 3 * HALF:4 * HALF].transpose(1, 0, 2).reshape(ar, D)]
    reshape x9 -> x3, local copies, waits for them, and re-layouts: 2.8 us -> 0.09 us  [the longest x2 0.05 us: body(): w_qkv.reshape(ar, 3, 2, 3, 128).transpose(2, 0, 3, 1, 4)]
    unnamed x32 -> x29, local copies, waits for them, and re-layouts: 4.83 us -> 7.1 us
    pallas_call x0 -> x3, local copies, waits for them, and re-layouts: none -> 2.07 us  [unpack(): pl.pallas_call(functools.partial(unpack_kernel, sh), name='unpack', out_s...]
where the time goes in v2:
time: 149 us
  Pallas kernels  136 us (91%)
  local copies, waits for them, and re-layouts  10.1 us (7%)
    pallas_call x1, Pallas kernels, layer(): pl.pallas_call(functools.partial(kernel, sh, names), name='layer', out_sh...  135 us
    unnamed x29, local copies, waits for them, and re-layouts  7.1 us

profile of v2, /device:TPU:1, one launch (start us, length us, event | category | flops | bytes accessed | tf_op | source)
XLA Modules:
  0.0 148.8 jit_solution(8574075650477771852)
XLA Ops:
  0.7 0.6 copy-done.11
  1.3 0.1 copy.33
  1.4 0.1 copy.34
  1.5 0.1 reshape.38
  1.6 0.1 maximum_bitcast_fusion.1
  1.7 0.6 pad_convert_fusion.refs_2_
  2.4 0.1 copy-done.5
  2.6 0.7 copy-done.6
  3.3 0.7 copy-done.7
  4.1 0.1 maximum_bitcast_fusion
  4.1 0.1 copy.36
  4.3 0.6 pad.22.refs_4_
  5.0 0.0 copy-done.9
  5.0 0.7 fusion.4.refs_3_
  5.7 135.2 %layer.1 = (bf16[2,128,768]{2,1,0:T(8,128)(2,1)}, f32[2,8,768]{2,1,0:T(8,128)}, bf16[2,128,768]{2,1,0:T(8,128)(2,1)}, f32[2,8,1664]{2,1,0:T(8,128)}, f32[2,24,768]{2,1,0:T(8,128)}) custom-call(bf16[2,128,768]{2,1,0:T(8,128)(2,1)} %refs_0_.1, bf16[2,128,768]{2,1,0:T(8,128)(2,1)} %refs_1_.1, f32[2,8,768]{2,1,0:T(8,128)} %pad_convert_fusion.refs_2_, ...), custom_call_target="tpu_custom_call" | custom-call | tf_op jit(solution)/shard_map/layer/pallas_call | solution.py:859
  140.9 1.0 copy-done
  141.9 1.0 copy-done.1
  142.9 0.9 copy-done.2
  143.8 0.9 copy-done.3
  144.7 0.8 copy-done.4
  145.5 1.2 unpack.1
  146.7 0.7 copy.38
  147.4 0.6 copy.37
  148.0 0.8 copy.39
  (24 shorter events, 0.2 us)
Async XLA Ops:
  0.6 0.7 copy-start.11
  0.7 0.8 copy-start.12
  0.7 0.9 copy-start.10
  0.7 1.0 copy-start.8
  1.7 0.8 copy-start.5
  2.5 0.8 copy-start.6
  3.3 0.8 copy-start.7
  4.3 0.7 copy-start.9
  140.9 1.0 copy-start
  141.9 1.0 copy-start.1
  142.9 0.9 copy-start.2
  143.8 0.9 copy-start.3
  144.7 0.8 copy-start.4

commit v3 on v2

--- a/solution.py
+++ b/solution.py
@@ -66,7 +66,11 @@
     for kind in range(2):
         for i in range(MEM):
             small[16 + 16 * kind + (i // 5) * 8 + i % 5, 4 + MEM * kind + i] = 1
-    return pack, small
+    places = np.zeros((4, MEM, SMALL), np.float32)
+    for kind, (rows, first) in enumerate(((2, 0), (2, 2), (MEM, 4), (MEM, 4 + MEM))):
+        for i in range(rows):
+            places[kind, i, first + i] = 1
+    return pack, small, places
 
 
 def norm_forward(inputs, gain, offset):
@@ -94,6 +98,9 @@
 def scratch_of(sh):
     nz, ny, br = sh.nz, sh.ny, sh.brows
     s = {
+        "pk": ((2, sh.pr, ACOLS), BF16),
+        "ff": ((2, sh.fr, D), BF16),
+        "gms": ((2, 8, D), F32),
         "p1": ((2, sh.pr, ACOLS), BF16),
         "p2": ((TP, 2 * sh.pc, ACOLS), BF16),
         "f1": ((2, sh.fr, D), BF16),
@@ -173,7 +180,7 @@
     jobs.append(("a0", zy, slice(0, HALF), zy))
     jobs.append(("a1", yz, slice(HALF, 2 * HALF), zy))
     jobs.append(("a2", zy, slice(2 * HALF, 2 * HALF + 256), zy))
-    jobs.append(("a3", yz, slice(2 * HALF + 256, 3 * HALF), zy))
+    jobs.append(("a3", zy, slice(2 * HALF + 256, 3 * HALF), zy))
     jobs.append(("as", yz, slice(4 * HALF, ACOLS), zy))
     return jobs
 
@@ -191,11 +198,12 @@
 
 
 def kernel(sh, names, *refs):
-    xin, gin, gmem, pk, ff, packsel, smallsel = refs[:7]
-    hout, mout, dxo, gao, gfo = refs[7:12]
-    b = dict(zip(names, refs[12 : 12 + len(names)]))
-    ssem, rsem, xsem, lsem = refs[12 + len(names) :]
-    nz, ny, br, wr, pr = sh.nz, sh.ny, sh.brows, sh.wrows, sh.pr
+    xin, gin, gmem, wq, wp, gain_in, bias_in, token_in, up_in, down_in, packsel, smallsel, places = refs[:13]
+    hout, mout, dxo, gao, gfo = refs[13:18]
+    b = dict(zip(names, refs[18 : 18 + len(names)]))
+    ssem, rsem, xsem, lsem = refs[18 + len(names) :]
+    nz, ny, br, wr, ar = sh.nz, sh.ny, sh.brows, sh.wrows, sh.arows
+    pk, ff, gms = b["pk"], b["ff"], b["gms"]
 
     dp = lax.axis_index("dp")
     x = lax.axis_index("tp")
@@ -256,6 +264,25 @@
             peers.append(moved(axis, o))
     for peer in peers:
         pl.semaphore_signal(barrier, inc=1, device_id=peer, device_id_type=MESH)
+
+    small = dot(gain_in[...], places[0, :2], TN) + dot(bias_in[...], places[1, :2], TN)
+    small = small + dot(token_in[:, 0], places[2]) + dot(token_in[:, 1], places[3])
+    small = small.astype(BF16)
+    pk[...] = jnp.zeros(pk.shape, BF16)
+    ff[...] = jnp.zeros(ff.shape, BF16)
+    gms[...] = jnp.zeros(gms.shape, F32)
+    for h in range(2):
+        for p in range(3):
+            for i in range(3):
+                first = D * i + HALF * h + 128 * p
+                pk[h, :ar, HALF * p + 128 * i : HALF * p + 128 * (i + 1)] = wq[:, first : first + 128]
+        pk[h, :ar, WO : WO + HALF] = wp[:, HALF * h : HALF * (h + 1)]
+        pk[h, :ar, 4 * HALF :] = small
+        for j in range(3):
+            cols = slice(HALF * h + 128 * j, HALF * h + 128 * (j + 1))
+            ff[h, :wr, 256 * j : 256 * j + 128] = up_in[:, cols]
+            ff[h, :wr, 256 * j + 128 : 256 * j + 256] = down_in[:, cols]
+        gms[h, 0:5] = gmem[:, h].astype(F32)
     pl.semaphore_wait(barrier, len(peers))
 
     pk_local = local(pk.at[core], b["p1"].at[core])
@@ -316,7 +343,7 @@
                     2 * s + j,
                 )
             to_device(
-                gmem.at[s], b["gm"].at[x % 2], (chip_of(core, s), x // 2), xsem.at[2, x % 2], 2, s
+                gms.at[s], b["gm"].at[x % 2], (chip_of(core, s), x // 2), xsem.at[2, x % 2], 2, s
             )
 
     def part_of(job, step, place, half=None):
@@ -610,22 +637,11 @@
     df_swap = remote(b["dfb"].at[own_rows], b["dfb"].at[own_rows], sibling)
     arrived([df_swap])
 
-    for t in range(2):
-        b["du"][t] = (dot(b["dfb"][...], down_weight(t)) * b["sl"][t].astype(F32)).astype(BF16)
-
-    def partial_up(rows):
-        return sum(dot(b["du"][t, rows], up_weight(t), NT) for t in range(2))
-
     def weight_grad(name, left, right):
         for t in range(2):
             part = dot(left, b[right][t], TN).astype(BF16)
             for i in range(2):
                 b[name][2 * t + i] = part[:, HALF * i : HALF * (i + 1)].reshape(nz, ny, br, HALF)
-
-    b["dhs"][...] = partial_up(other_rows).astype(BF16)
-    dh_swap = remote(b["dhs"], b["dhr"], sibling)
-    b["dz"][...] = b["dz"][...] + partial_up(own_rows)
-    weight_grad("gt", b["dfb"][...], "gl")
 
     def pick(axes, axis, place):
         return tuple(place if a == axis else slice(None) for a in axes)
@@ -673,8 +689,18 @@
             scatter_send(n, step + 1)
 
     down_names, up_names = ("t0", "t1", "t2"), ("i0", "i1", "i2")
+    weight_grad("gt", b["dfb"][...], "gl")
     for n in down_names:
         scatter_send(n, 0)
+    for t in range(2):
+        b["du"][t] = (dot(b["dfb"][...], down_weight(t)) * b["sl"][t].astype(F32)).astype(BF16)
+
+    def partial_up(rows):
+        return sum(dot(b["du"][t, rows], up_weight(t), NT) for t in range(2))
+
+    b["dhs"][...] = partial_up(other_rows).astype(BF16)
+    dh_swap = remote(b["dhs"], b["dhr"], sibling)
+    b["dz"][...] = b["dz"][...] + partial_up(own_rows)
     weight_grad("gi", b["h1b"][...], "du")
     for n in up_names:
         scatter_send(n, 0)
@@ -712,9 +738,6 @@
     b["gos"][...] = proj_grad(other)
     go_swap = remote(b["gos"], wo_part(core), sibling)
     wo_part(core)[...] = proj_grad(core)
-    scatter_on(down_names, 0)
-    arrived([go_swap])
-    scatter_send("aw", 0)
 
     def backward_pair(p):
         qp, kp, vp = (b["qkv"][3 * p + i] for i in range(3))
@@ -746,12 +769,14 @@
 
     backward_pair(0)
     attention_grad(0)
+    arrived([go_swap])
+    scatter_send("aw", 0)
     scatter_send("a0", 0)
-    scatter_on(up_names, 0)
+    scatter_on(down_names, 0)
     backward_pair(1)
     attention_grad(1)
     scatter_send("a1", 0)
-    scatter_on(down_names, 1)
+    scatter_on(up_names, 0)
     backward_pair(2)
     attention_grad(2)
     scatter_send("a2", 0)
@@ -788,8 +813,9 @@
     b["ga"][:, :, :, 4 * HALF :] = small_grads.reshape(nz, ny, br, SMALL)
     scatter_send("as", 0)
     attention_names = ("aw", "a0", "a1", "a2", "a3", "as")
+    scatter_on(down_names, 1)
+    scatter_on(attention_names, 0)
     scatter_on(up_names, 1)
-    scatter_on(attention_names, 0)
 
     def last_rows(names, first_col):
         for j, n in enumerate(names):
@@ -798,12 +824,12 @@
             b["sf"][0, :, cols] = total[:wr]
             b["sf"][1, :, cols] = total[wr:]
 
-    last_rows(down_names, HALF)
     for n in attention_names:
         cols = scatters[n][2]
         spread = dot(packsel[...], scatter_sum(n, 1).astype(BF16), TN).astype(BF16)
         b["e3"][:, :, cols] = spread.reshape(TP, 2 * sh.pc, cols.stop - cols.start)
     steps = [remote(b["e3"].at[(x + o) % TP], b["r3"].at[o - 1], moved("x", o)) for o in range(1, TP)]
+    last_rows(down_names, HALF)
     last_rows(up_names, 0)
     sf_local = local(b["sf"].at[core], gfo.at[core])
     sf_swap = remote(b["sf"].at[other], gfo.at[core], sibling)
@@ -845,7 +871,7 @@
 
 
 def layer(sh, arrays):
-    pack, small = selections(sh)
+    constants = [jnp.asarray(a, BF16) for a in selections(sh)]
     table = scratch_of(sh)
     names = list(table)
     vmem = pl.BlockSpec(memory_space=pltpu.VMEM)
@@ -860,8 +886,8 @@
         functools.partial(kernel, sh, names),
         name="layer",
         out_shape=outs,
-        in_specs=[vmem] * 7,
-        out_specs=[vmem] * len(outs),
+        in_specs=[pl.BlockSpec(memory_space=pl.ANY)] * 2 + [vmem] * 11,
+        out_specs=[pl.BlockSpec(memory_space=pl.ANY), vmem] * 2 + [vmem],
         scratch_shapes=[pltpu.VMEM(*table[n]) for n in names]
         + [
             pltpu.SemaphoreType.DMA((200,)),
@@ -872,14 +898,15 @@
         compiler_params=pltpu.CompilerParams(
             collective_id=0, has_side_effects=True, vmem_limit_bytes=64 * 2**20 - 2**17
         ),
-    )(*arrays, jnp.asarray(pack, BF16), jnp.asarray(small, BF16))
+    )(*arrays, *constants)
 
 
 def unpack_kernel(sh, hout, mout, dxo, gao, gfo, *outs):
     hidden, memory, grad_in, gq, gp, gains, biases, tokens, gi, gt = outs
     ar = sh.arows
     hidden[...] = hout[...]
-    memory[...] = mout[...][:, :5].astype(BF16)
+    for i in range(2):
+        memory[:, i] = mout[i, :5].astype(BF16)
     grad_in[...] = dxo[...].astype(F32)
     for h in range(2):
         for p in range(3):
@@ -889,27 +916,28 @@
                 gq[:, to : to + 128] = gao[h, :ar, first : first + 128]
         gp[:, HALF * h : HALF * (h + 1)] = gao[h, :ar, WO : WO + HALF]
         gi[:, HALF * h : HALF * (h + 1)] = gfo[h, :, :HALF]
-        gt[HALF * h : HALF * (h + 1), :] = gfo[h, :, HALF:].T
-    small = (gao[0, :, 4 * HALF :] + gao[1, :, 4 * HALF :]).T[:, :ar]
-    gains[...] = small[0:2]
-    biases[...] = small[2:4]
+        gt[:, HALF * h : HALF * (h + 1)] = gfo[h, :, HALF:]
+    small = gao[0, :, 4 * HALF :] + gao[1, :, 4 * HALF :]
+    turned = small.T[:, :ar]
+    gains[...] = turned[0:2]
+    biases[...] = turned[2:4]
     for kind in range(2):
-        tokens[kind] = small[4 + MEM * kind : 4 + MEM * (kind + 1)]
+        tokens[:, kind] = small[:ar, 4 + MEM * kind : 4 + MEM * (kind + 1)]
 
 
 def unpack(sh, *arrays):
     ar, wr = sh.arows, sh.wrows
     shapes = [
         ((2, 128, D), BF16),
-        ((2, 5, D), BF16),
+        ((5, 2, D), BF16),
         ((2, 128, D), F32),
         ((ar, 3 * D), F32),
         ((ar, D), F32),
         ((2, ar), F32),
         ((2, ar), F32),
-        ((2, MEM, ar), F32),
+        ((ar, 2, MEM), F32),
         ((wr, D), F32),
-        ((D, wr), F32),
+        ((wr, D), F32),
     ]
     vmem = pl.BlockSpec(memory_space=pltpu.VMEM)
     return pl.pallas_call(
@@ -918,7 +946,7 @@
         out_shape=[jax.ShapeDtypeStruct(*one) for one in shapes],
         in_specs=[vmem] * 5,
         out_specs=[vmem] * len(shapes),
-        compiler_params=pltpu.CompilerParams(vmem_limit_bytes=32 * 2**20),
+        compiler_params=pltpu.CompilerParams(vmem_limit_bytes=64 * 2**20 - 2**17),
     )(*arrays)
 
 
@@ -936,20 +964,20 @@
     grad_hidden,
     grad_memory,
 ):
-    ar, wr = sh.arows, sh.wrows
-    small = jnp.concatenate([norm_gains, norm_biases, memory_tokens.reshape(2 * MEM, ar)], 0).T
-    small = jnp.pad(small, ((0, 0), (0, SMALL - small.shape[1])))
-    by_half = w_qkv.reshape(ar, 3, 2, 3, 128).transpose(2, 0, 3, 1, 4).reshape(2, ar, 3 * HALF)
-    proj = w_attn_out.reshape(ar, 2, HALF).transpose(1, 0, 2)
-    pk = jnp.concatenate([by_half, proj, jnp.broadcast_to(small, (2, ar, SMALL))], 2)
-    pk = jnp.pad(pk, ((0, 0), (0, sh.pr - ar), (0, 0)))
-    both = jnp.stack([w_in.reshape(wr, 2, 3, 128), w_out.T.reshape(wr, 2, 3, 128)], 3)
-    ff = both.transpose(1, 0, 2, 3, 4).reshape(2, wr, D)
-    ff = jnp.pad(ff, ((0, 0), (0, sh.fr - wr), (0, 0)))
-    gmem = jnp.pad(grad_memory.astype(F32), ((0, 0), (0, 3), (0, 0)))
-    hout, mout, dxo, gao, gfo = layer(sh, (hidden_in, grad_hidden, gmem, pk, ff))
-
-    return unpack(sh, hout, mout, dxo, gao, gfo)
+    arrays = (
+        hidden_in,
+        grad_hidden,
+        grad_memory.transpose(1, 0, 2),
+        w_qkv,
+        w_attn_out,
+        norm_gains,
+        norm_biases,
+        memory_tokens.transpose(2, 0, 1),
+        w_in,
+        w_out.T,
+    )
+    hidden, memory, *middle, tokens, gi, gt = unpack(sh, *layer(sh, arrays))
+    return hidden, memory.transpose(1, 0, 2), *middle, tokens.transpose(1, 2, 0), gi, gt.T
 
 
 def solution(mesh):

time: 149 us -> 131 us (0.88)
  local copies, waits for them, and re-layouts: 10.1 us -> 0 us
  Pallas kernels: 136 us -> 130 us
    unnamed x29 -> x0, local copies, waits for them, and re-layouts: 7.1 us -> none
    pallas_call x1, Pallas kernels: 135 us -> 128 us  [layer(): pl.pallas_call(functools.partial(kernel, sh, names), name='layer', out_sh...]
    pallas_call x3 -> x0, local copies, waits for them, and re-layouts: 2.07 us -> none  [unpack(): pl.pallas_call(functools.partial(unpack_kernel, sh), name='unpack', out_s...]
where the time goes in v3:
time: 131 us
  Pallas kernels  130 us (99%)
    pallas_call x1, Pallas kernels, layer(): pl.pallas_call(functools.partial(kernel, sh, names), name='layer', out_sh...  128 us

profile of v3, /device:TPU:1, one launch (start us, length us, event | category | flops | bytes accessed | tf_op | source)
XLA Modules:
  0.0 131.3 jit_solution(16127918936387328646)
XLA Ops:
  0.6 128.1 %layer.1 = (bf16[2,128,768]{2,1,0:T(8,128)(2,1)}, f32[2,8,768]{2,1,0:T(8,128)}, bf16[2,128,768]{2,1,0:T(8,128)(2,1)}, f32[2,8,1664]{2,1,0:T(8,128)}, f32[2,24,768]{2,1,0:T(8,128)}) custom-call(bf16[2,128,768]{2,1,0:T(8,128)(2,1)} %refs_0_.1, bf16[2,128,768]{2,1,0:T(8,128)(2,1)} %refs_1_.1, bf16[5,2,768]{2,1,0:T(2,128)(2,1)} %bitcast.7, ...), custom_call_target="tpu_custom_call" | custom-call | tf_op jit(solution)/shard_map/layer/pallas_call | solution.py:885
  128.8 2.3 %unpack.1 = (bf16[2,128,768]{2,1,0:T(8,128)(2,1)}, bf16[5,2,768]{2,1,0:T(2,128)(2,1)}, f32[2,128,768]{2,1,0:T(8,128)}, f32[6,2304]{1,0:T(8,128)}, f32[6,768]{1,0...) custom-call(bf16[2,128,768]{2,1,0:T(8,128)(2,1)} %get-tuple-element., ...), custom_call_target="tpu_custom_call" | custom-call | tf_op jit(solution)/shard_map/unpack/pallas_call | solution.py:943
